TPU v7x, 128 devices: a whole 4x4x4 slice. The times are simulated.
128 devices in a mesh: batch: 8 (over x_lo, y), lat: 16 (over x_hi, z, core).
Axes of the slice: x: 4 (x_hi: 2, x_lo: 2; x = x_hi * 2 + x_lo), y: 4, z: 4, core: 2. Of those that a mesh axis runs over, the one named last changes fastest.
Arguments:
- field: bfloat16 [16, 96, 180, 768], P('batch', 'lat'), may hold values from -6 to 6
- cotangent: bfloat16 [16, 96, 180, 768], P('batch', 'lat'), may hold values from -6 to 6
- weight_one: float32 [2, 8, 96, 96], replicated, may hold values from -0.4375 to 0.4375
- bias_one: float32 [2, 8, 96], replicated, may hold values from -2 to 2
- weight_two: float32 [2, 8, 96, 96], replicated, may hold values from -0.4375 to 0.4375
- bias_two: float32 [2, 8, 96], replicated, may hold values from -2 to 2
Outputs:
- field_grad: bfloat16 [16, 96, 180, 768], P('batch', 'lat')
- weight_one_grad: float32 [2, 8, 96, 96], replicated
- bias_one_grad: float32 [2, 8, 96], replicated
- weight_two_grad: float32 [2, 8, 96, 96], replicated
- bias_two_grad: float32 [2, 8, 96], replicated
All inputs are finite; a program needn't handle non-finite values.
Results may differ from a plain program's by a relative error of at most 0.017.
Values may be sent and summed in bfloat16 or wider, within the bound.
A program may use at most 192 MiB of HBM per device.

v0:
```python
import math

import jax
import jax.numpy as jnp
from jax import lax
from jax.sharding import PartitionSpec as P

KP = 96


shrink_width = 0.25


def lon_tables(width, slots):
    wpos = jnp.arange(width, dtype=jnp.int32)
    kpos = jnp.arange(slots, dtype=jnp.int32)
    phase = wpos[:, None] * kpos[None, :] % width
    angle = phase.astype(jnp.float32) * (2.0 * math.pi / width)
    valid = (kpos <= width // 2).astype(jnp.float32)[None, :]
    factor = 1.0 / math.sqrt(width)
    cosine = jnp.cos(angle) * valid * factor
    sine = jnp.sin(angle) * valid * factor
    forward = jnp.stack([cosine, -sine], axis=1).astype(jnp.bfloat16)
    weight = jnp.where((kpos == 0) | (kpos == width // 2), 1.0, 2.0).astype(jnp.float32)[None, :]
    inverse = jnp.stack([(cosine * weight).T, (-sine * weight).T], axis=0).astype(jnp.bfloat16)
    return (forward, inverse)


def lat_table(count, sign):
    pos = jnp.arange(count, dtype=jnp.int32)
    phase = pos[:, None] * pos[None, :] % count
    angle = phase.astype(jnp.float32) * (2.0 * math.pi / count)
    factor = 1.0 / math.sqrt(count)
    cosine = jnp.cos(angle) * factor
    sine = jnp.sin(angle) * (factor * sign)
    upper = jnp.stack([cosine, -sine], axis=-1)
    lower = jnp.stack([sine, cosine], axis=-1)
    return jnp.stack([upper, lower], axis=1).astype(jnp.bfloat16)


def block_matrix(weights):
    real_part = weights[0]
    imag_part = weights[1]
    first = jnp.stack([real_part, imag_part], axis=2)
    second = jnp.stack([-imag_part, real_part], axis=2)
    return jnp.stack([first, second], axis=0)


def spectral_mix(spectra, weight_one, bias_one, weight_two, bias_two, lat_fwd, lat_inv):
    samples, lats, _, slots, chans = spectra.shape
    blocks = bias_one.shape[1]
    size = bias_one.shape[2]
    mixed = jnp.einsum("mphq,bhqkc->bmpkc", lat_fwd, spectra, preferred_element_type=jnp.float32)
    mixed = mixed.reshape(samples, lats, 2, slots, blocks, size)
    first = jnp.einsum(
        "bmqkni,qnipj->bmpknj", mixed, block_matrix(weight_one), precision=lax.Precision.HIGHEST
    )
    first = first + bias_one[None, None, :, None, :, :]
    hidden = jax.nn.gelu(first, approximate=True)
    second = jnp.einsum(
        "bmqkni,qnipj->bmpknj", hidden, block_matrix(weight_two), precision=lax.Precision.HIGHEST
    )
    second = second + bias_two[None, None, :, None, :, :]
    shrunk = second - shrink_width * jnp.tanh(second / shrink_width)
    shrunk = shrunk.reshape(samples, lats, 2, slots, chans).astype(jnp.bfloat16)
    result = jnp.einsum("hpmq,bmqkc->bhpkc", lat_inv, shrunk, preferred_element_type=jnp.float32)
    return result.astype(jnp.bfloat16)


def local(field, cotangent, weight_one, bias_one, weight_two, bias_two):
    samples, local_lats, width, chans = field.shape
    lat_count = local_lats * lax.axis_size("lat")
    lon_fwd, lon_inv = lon_tables(width, KP)
    lat_fwd = lat_table(lat_count, -1.0)
    lat_inv = lat_table(lat_count, 1.0)

    def mixing(spec, first_w, first_b, second_w, second_b):
        return spectral_mix(spec, first_w, first_b, second_w, second_b, lat_fwd, lat_inv)

    spectra = jnp.einsum(
        "wqk,bhwc->bhqkc", lon_fwd, field, preferred_element_type=jnp.float32
    ).astype(jnp.bfloat16)
    spec_cot = jnp.einsum(
        "qkw,bhwc->bhqkc", lon_inv, cotangent, preferred_element_type=jnp.float32
    ).astype(jnp.bfloat16)
    owned, owned_cot = (
        lax.all_to_all(spectra, "lat", split_axis=3, concat_axis=1, tiled=True),
        lax.all_to_all(spec_cot, "lat", split_axis=3, concat_axis=1, tiled=True),
    )
    _, pullback = jax.vjp(mixing, owned, weight_one, bias_one, weight_two, bias_two)
    grads = pullback(owned_cot)
    returned = lax.all_to_all(grads[0], "lat", split_axis=1, concat_axis=3, tiled=True)
    field_grad = jnp.einsum(
        "wqk,bhqkc->bhwc", lon_fwd, returned, preferred_element_type=jnp.float32
    ).astype(jnp.bfloat16)
    totals = lax.psum((grads[1], grads[2], grads[3], grads[4]), ("batch", "lat"))
    total_samples = samples * lax.axis_size("batch")
    factor = 1.0 / math.sqrt(total_samples * lat_count * (width // 2 + 1))
    return (
        field_grad,
        totals[0] * factor,
        totals[1] * factor,
        totals[2] * factor,
        totals[3] * factor,
    )


def solution(mesh):
    in_specs = (P("batch", "lat", None, None), P("batch", "lat", None, None), P(), P(), P(), P())
    out_specs = (P("batch", "lat", None, None), P(), P(), P(), P())
    return jax.shard_map(local, mesh=mesh, in_specs=in_specs, out_specs=out_specs, check_vma=False)
```

profile of v0, /device:TPU:1, one launch (start us, length us, event | category | flops | bytes accessed | tf_op | source)
XLA Modules:
  0.0 498.9 jit_solution(13357959654223816315)
XLA Ops:
  8.3 3.1 convert_bitcast_fusion.1
  11.3 5.4 %copy.141 = bf16[2,6,2,96,768]{4,2,1,0,3:T(2,128)(2,1)} copy(bf16[2,6,2,96,768]{4,3,1,0,2:T(8,128)(2,1)S(1)} %convert_bitcast_fusion.1) | data formatting | bytes 7077888 | tf_op jit(solution)/shard_map/convert_element_type | solution.py:82
  16.7 9.3 %all-to-all-start.1 = ((bf16[2,6,2,96,768]{4,2,1,0,3:T(2,128)(2,1)}), bf16[2,6,2,96,768]{4,2,1,0,3:T(2,128)(2,1)S(1)}, u32[]{:S(2)}, u32[]{:S(2)}) async-start(bf16[2,6,2,96,768]{4,2,1,0,3:T(2,128)(2,1)} %copy.141), calls=%async_computation.1 | async-start | bytes 7077888 | tf_op jit(solution)/shard_map/all_to_all | solution.py:87
  26.5 3.1 convert_bitcast_fusion.2
  29.6 5.5 %copy.132 = bf16[2,6,2,96,768]{4,2,1,0,3:T(2,128)(2,1)} copy(bf16[2,6,2,96,768]{4,3,1,0,2:T(8,128)(2,1)S(1)} %convert_bitcast_fusion.2) | data formatting | bytes 7077888 | tf_op jit(solution)/shard_map/convert_element_type | solution.py:85
  35.0 36.7 %all-to-all-done.1 = bf16[2,6,2,96,768]{4,2,1,0,3:T(2,128)(2,1)S(1)} async-done(((bf16[2,6,2,96,768]{4,2,1,0,3:T(2,128)(2,1)}), bf16[2,6,2,96,768]{4,2,1,0,3:T(2,128)(2,1)S(1)}, u32[]{:S(2)}, u32[]{:S(2)}) %all-to-all-start.1) | async-done | bytes 3538976 | tf_op jit(solution)/shard_map/all_to_all | solution.py:87
  71.7 12.5 %all-to-all-start = ((bf16[2,6,2,96,768]{4,2,1,0,3:T(2,128)(2,1)}), bf16[2,6,2,96,768]{4,2,1,0,3:T(2,128)(2,1)}, u32[]{:S(2)}, u32[]{:S(2)}) async-start(bf16[2,6,2,96,768]{4,2,1,0,3:T(2,128)(2,1)} %copy.132), calls=%async_computation | async-start | bytes 7077888 | tf_op jit(solution)/shard_map/all_to_all | solution.py:88
  84.3 1.3 copy.149
  87.5 1.1 fusion.129
  88.6 1.2 slice_bitcast_fusion.5
  89.8 1.3 maximum_bitcast_fusion.2
  91.1 1.0 fusion.128
  92.1 1.2 slice_bitcast_fusion.7
  93.3 1.3 maximum_bitcast_fusion
  94.6 2.4 copy.143
  97.1 4.0 fusion.57
  101.1 10.4 %reshape.477 = f32[2,96,2,6,8,96]{5,4,1,2,3,0:T(8,128)} reshape(f32[2,96,2,6,768]{4,1,2,3,0:T(8,128)} %fusion.57) | data formatting | bytes 14155776 | tf_op jit(solution)/shard_map/jvp()/reshape | solution.py:54
  111.5 18.3 %all-to-all-done = bf16[2,6,2,96,768]{4,2,1,0,3:T(2,128)(2,1)} async-done(((bf16[2,6,2,96,768]{4,2,1,0,3:T(2,128)(2,1)}), bf16[2,6,2,96,768]{4,2,1,0,3:T(2,128)(2,1)}, u32[]{:S(2)}, u32[]{:S(2)}) %all-to-all-start) | async-done | bytes 3538976 | tf_op jit(solution)/shard_map/all_to_all | solution.py:88
  129.8 4.4 copy.134
  134.3 4.0 convert_bitcast_fusion
  138.3 10.5 %reshape.480 = f32[2,96,2,6,8,96]{5,4,1,2,3,0:T(8,128)} reshape(f32[2,96,2,6,768]{4,1,2,3,0:T(8,128)} %convert_bitcast_fusion) | data formatting | bytes 14155776 | tf_op jit(solution)/shard_map/transpose(jvp())/reshape | solution.py:65
  148.9 16.4 %fusion.32 = f32[8,2,96,2,96,6,1]{2,4,6,5,3,1,0:T(8,128)S(1)} fusion(f32[2,96,2,6,8,96,1]{5,4,1,2,3,0,6:T(8,128)} %bitcast.297, f32[1,8,96,2,96]{4,2,0,3,1:T(8,128)S(1)} %copy-done.3, f32[1,8,96,2,96]{4,2,0,3,1:T(8,128)S(1)} %copy-done.2), kind=kOutput, calls=%fused_computation.43 | convolution fusion | flops 4077158400 | bytes 15335424 | tf_op jit(solution)/shard_map/jvp(bmqkni,qnipj->bmpknj)/dot_general | solution.py:55
  165.3 19.5 %fusion.131 = (f32[2,8,96]{2,0,1:T(2,128)}, f32[2,96,2,6,8,96]{5,1,3,0,2,4:T(8,128)}) fusion(f32[2,8,96]{2,0,1:T(2,128)S(1)} %copy-done.14, f32[1,8,96,2,96]{4,2,0,3,1:T(8,128)S(1)} %copy-done.5, f32[1,8,96,2,96]{4,2,0,3,1:T(8,128)S(1)} %copy-done.4, f32[2,96,2,6,8,96]{5,4,1,2,3,0:T(8,128)S(1)} %copy-done.1, f32[8,2,96,2,96,6,1]{2,4,6,5,3,1,0:T(8,128)S(1)} %fusion.32, ...), kind=kOutput, calls=%fused_computation.177 | convolution fusion | flops 4112546304 | bytes 22431744 | tf_op jit(solution)/shard_map/jvp(bmqkni,qnipj->bmpknj)/dot_general | solution.py:60
  184.8 21.6 %fusion.74 = f32[2,8,96,2,96]{2,4,1,3,0:T(8,128)S(1)} fusion(f32[2,96,2,6,8,96]{5,1,3,0,2,4:T(8,128)} %get-tuple-element.54, f32[8,2,96,2,96,6,1]{2,4,6,5,3,1,0:T(8,128)} %copy-done, f32[2,8,96]{2,0,1:T(2,128)S(1)} %copy.147), kind=kOutput, calls=%fused_computation.79 | convolution fusion | flops 4092788736 | bytes 15341568 | tf_op jit(solution)/shard_map/transpose(jvp(bmqkni,qnipj->bmpknj))/dot_general | solution.py:60
  206.4 21.3 %fusion.12 = (f32[8,2,96,2,96,6]{2,4,5,3,1,0:T(8,128)}, f32[8,2,96,6,2,96,1]{5,2,6,3,1,4,0:T(8,128)}) fusion(f32[8,2,96,2,96,6,1]{2,4,6,5,3,1,0:T(8,128)} %copy-done, f32[8,2,96]{2,1,0:T(2,128)S(1)} %copy-done.13, f32[2,96,2,6,8,96]{5,1,3,0,2,4:T(8,128)} %get-tuple-element.54, f32[1,8,96,2,96]{4,2,0,3,1:T(8,128)S(1)} %copy-done.5, ...), kind=kOutput, calls=%fused_computation.16 | convolution fusion | flops 4112547840 | bytes 29497344 | tf_op jit(solution)/shard_map/transpose(jvp(bmqkni,qnipj->bmpknj))/dot_general | solution.py:60
  227.7 22.2 %fusion.79 = f32[2,8,96,2,96]{2,4,0,3,1:T(8,128)S(1)} fusion(f32[2,96,2,6,8,96,1]{5,4,1,2,3,0,6:T(8,128)} %bitcast.298, f32[8,2,96,2,96,6]{2,4,5,3,1,0:T(8,128)} %get-tuple-element.51), kind=kOutput, calls=%fused_computation.80 | convolution fusion | flops 4076863488 | bytes 15335424 | tf_op jit(solution)/shard_map/transpose(jvp(bmqkni,qnipj->bmpknj))/dot_general | solution.py:55
  250.1 0.8 fusion.90
  250.9 0.8 fusion.88
  251.7 11.2 %fusion.45 = bf16[2,96,2,6,8,96]{5,1,2,3,0,4:T(8,128)(2,1)S(1)} fusion(f32[8,2,96,2,96,6]{2,4,5,3,1,0:T(8,128)} %get-tuple-element.51, f32[1,8,96,2,96]{4,2,0,3,1:T(8,128)S(1)} %copy-done.3, f32[1,8,96,2,96]{4,2,0,3,1:T(8,128)S(1)} %copy-done.2), kind=kOutput, calls=%fused_computation.64 | convolution fusion | flops 4077158400 | bytes 11796480 | tf_op jit(solution)/shard_map/transpose(jvp(bmqkni,qnipj->bmpknj))/dot_general | solution.py:55
  262.9 1.2 slice_bitcast_fusion.1
  264.2 5.3 %copy.157 = bf16[2,96,2,6,8,96]{5,4,1,3,2,0:T(8,128)(2,1)} copy(bf16[2,96,2,6,8,96]{5,1,2,3,0,4:T(8,128)(2,1)S(1)} %fusion.45) | data formatting | bytes 7077888 | tf_op jit(solution)/shard_map/transpose(jvp(bmqkni,qnipj->bmpknj))/transpose | solution.py:55
  269.5 7.2 %reshape.478 = bf16[2,96,2,6,768]{4,1,3,2,0:T(8,128)(2,1)S(1)} reshape(bf16[2,96,2,6,8,96]{5,4,1,3,2,0:T(8,128)(2,1)} %copy.157) | data formatting | bytes 7077888 | tf_op jit(solution)/shard_map/transpose(jvp())/reshape | solution.py:54
  276.6 1.9 fusion.37
  278.6 5.5 %copy.160 = bf16[2,96,2,6,768]{4,2,3,0,1:T(2,128)(2,1)} copy(bf16[2,96,2,6,768]{4,1,2,3,0:T(8,128)(2,1)S(1)} %fusion.37) | data formatting | bytes 7077888 | tf_op jit(solution)/shard_map/transpose(jvp(mphq,bhqkc->bmpkc))/convert_element_type | solution.py:53
  284.1 12.3 %all-to-all-start.2 = ((bf16[2,96,2,6,768]{4,2,3,0,1:T(2,128)(2,1)}), bf16[2,96,2,6,768]{4,2,3,0,1:T(2,128)(2,1)S(1)}, u32[]{:S(2)}, u32[]{:S(2)}) async-start(bf16[2,96,2,6,768]{4,2,3,0,1:T(2,128)(2,1)} %copy.160), calls=%async_computation.2 | async-start | bytes 7077888 | tf_op jit(solution)/shard_map/all_to_all | solution.py:92
  296.4 1.4 fusion.87
  297.9 1.0 pad_add_fusion
  298.8 2.1 pad_add_fusion.1
  300.9 10.5 %fusion.6 = f32[2,8,96]{2,0,1:T(2,128)S(1)} fusion(f32[8,2,96,6,2,96,1]{5,2,6,3,1,4,0:T(8,128)} %get-tuple-element.52, f32[8,2,96,2,96,6,1]{2,4,6,5,3,1,0:T(8,128)} %copy-done, f32[2,8,96]{2,0,1:T(2,128)S(1)} %copy.147), kind=kLoop, calls=%fused_computation.10 | loop fusion | flops 37157376 | bytes 14168064 | tf_op jit(solution)/shard_map/transpose(jvp())/reduce_sum | solution.py:58
  311.4 90.2 %all-reduce.4 = (f32[2,8,96]{2,0,1:T(2,128)}, f32[2,8,96]{2,0,1:T(2,128)S(1)}) all-reduce(f32[2,8,96]{2,0,1:T(2,128)S(1)} %fusion.6, f32[2,8,96]{2,0,1:T(2,128)} %get-tuple-element.53), channel_id=1, replica_groups=mesh['batch'=8,'lat'=16] {'batch','lat'}, use_global_device_ids=true, to_apply=%region_2.3 | all-reduce | flops 3072 | bytes 24576 | tf_op jit(solution)/shard_map/psum | solution.py:96
  403.5 70.1 %all-reduce.8.cloned.1.call-done = (f32[2,8,96,96]{2,3,1,0:T(8,128)}, f32[2,8,96,96]{2,3,1,0:T(8,128)}) async-done(((f32[2,8,96,96]{2,3,1,0:T(8,128)}, f32[2,8,96,96]{2,3,1,0:T(8,128)}), (f32[2,8,96,96]{2,3,1,0:T(8,128)}, f32[2,8,96,96]{2,3,1,0:T(8,128)})) %all-reduce.8.cloned.1.call-update) | async-done | bytes 1179664 | tf_op jit(solution)/shard_map/psum | solution.py:96
  473.6 2.1 broadcast_multiply_fusion.1
  475.7 2.3 copy.173
  478.0 2.1 broadcast_multiply_fusion
  480.1 2.3 copy.175
  482.4 3.0 copy.162
  485.4 1.9 fusion.50
  487.3 4.3 copy.172
  (49 shorter events, 5.7 us)
Async XLA Ops:
  7.6 0.6 copy-start.8
  7.6 0.6 copy-start.9
  16.7 55.0 %all-to-all-start.1 = ((bf16[2,6,2,96,768]{4,2,1,0,3:T(2,128)(2,1)}), bf16[2,6,2,96,768]{4,2,1,0,3:T(2,128)(2,1)S(1)}, u32[]{:S(2)}, u32[]{:S(2)}) async-start(bf16[2,6,2,96,768]{4,2,1,0,3:T(2,128)(2,1)} %copy.141), calls=%async_computation.1 | async-start | bytes 7077888 | tf_op jit(solution)/shard_map/all_to_all | solution.py:87
  26.5 57.8 %copy-start.12 = (f32[2,8,96]{2,1,0:T(8,128)S(1)}, f32[2,8,96]{2,1,0:T(8,128)}, u32[]{:S(2)}) copy-start(f32[2,8,96]{2,1,0:T(8,128)} %param.9) | copy-start | bytes 18436
  71.7 58.1 %all-to-all-start = ((bf16[2,6,2,96,768]{4,2,1,0,3:T(2,128)(2,1)}), bf16[2,6,2,96,768]{4,2,1,0,3:T(2,128)(2,1)}, u32[]{:S(2)}, u32[]{:S(2)}) async-start(bf16[2,6,2,96,768]{4,2,1,0,3:T(2,128)(2,1)} %copy.132), calls=%async_computation | async-start | bytes 7077888 | tf_op jit(solution)/shard_map/all_to_all | solution.py:88
  87.5 9.5 %copy-start.6 = (bf16[96,1,96,2]{0,2,3,1:T(8,128)(2,1)}, bf16[96,1,96,2]{0,2,3,1:T(8,128)(2,1)S(1)}, u32[]{:S(2)}) copy-start(bf16[96,1,96,2]{0,2,3,1:T(8,128)(2,1)S(1)} %get-tuple-element.43) | copy-start | bytes 110596
  87.5 9.6 %copy-start.7 = (bf16[96,1,96,2]{0,2,3,1:T(8,128)(2,1)}, bf16[96,1,96,2]{0,2,3,1:T(8,128)(2,1)S(1)}, u32[]{:S(2)}) copy-start(bf16[96,1,96,2]{0,2,3,1:T(8,128)(2,1)S(1)} %get-tuple-element.44) | copy-start | bytes 110596
  101.1 33.2 %copy-start.10 = (bf16[96,1,96,2]{0,2,1,3:T(8,128)(2,1)S(1)}, bf16[96,1,96,2]{0,2,1,3:T(8,128)(2,1)}, u32[]{:S(2)}) copy-start(bf16[96,1,96,2]{0,2,1,3:T(8,128)(2,1)} %get-tuple-element.45) | copy-start | bytes 110596
  101.1 33.2 %copy-start.11 = (bf16[96,1,96,2]{0,2,1,3:T(8,128)(2,1)S(1)}, bf16[96,1,96,2]{0,2,1,3:T(8,128)(2,1)}, u32[]{:S(2)}) copy-start(bf16[96,1,96,2]{0,2,1,3:T(8,128)(2,1)} %get-tuple-element.46) | copy-start | bytes 110596
  138.3 10.5 %copy-start.2 = (f32[1,8,96,2,96]{4,2,0,3,1:T(8,128)S(1)}, f32[1,8,96,2,96]{4,2,0,3,1:T(8,128)}, u32[]{:S(2)}) copy-start(f32[1,8,96,2,96]{4,2,0,3,1:T(8,128)} %get-tuple-element.41) | copy-start | bytes 1769476
  138.3 10.5 %copy-start.3 = (f32[1,8,96,2,96]{4,2,0,3,1:T(8,128)S(1)}, f32[1,8,96,2,96]{4,2,0,3,1:T(8,128)}, u32[]{:S(2)}) copy-start(f32[1,8,96,2,96]{4,2,0,3,1:T(8,128)} %get-tuple-element.42) | copy-start | bytes 1769476
  148.8 16.4 %copy-start.1 = (f32[2,96,2,6,8,96]{5,4,1,2,3,0:T(8,128)S(1)}, f32[2,96,2,6,8,96]{5,4,1,2,3,0:T(8,128)}, u32[]{:S(2)}) copy-start(f32[2,96,2,6,8,96]{5,4,1,2,3,0:T(8,128)} %reshape.480) | copy-start | bytes 21233668
  148.8 16.4 %copy-start.4 = (f32[1,8,96,2,96]{4,2,0,3,1:T(8,128)S(1)}, f32[1,8,96,2,96]{4,2,0,3,1:T(8,128)}, u32[]{:S(2)}) copy-start(f32[1,8,96,2,96]{4,2,0,3,1:T(8,128)} %get-tuple-element.39) | copy-start | bytes 1769476
  148.8 16.4 %copy-start.5 = (f32[1,8,96,2,96]{4,2,0,3,1:T(8,128)S(1)}, f32[1,8,96,2,96]{4,2,0,3,1:T(8,128)}, u32[]{:S(2)}) copy-start(f32[1,8,96,2,96]{4,2,0,3,1:T(8,128)} %get-tuple-element.40) | copy-start | bytes 1769476
  148.9 16.4 %copy-start.14 = (f32[2,8,96]{2,0,1:T(2,128)S(1)}, f32[2,8,96]{2,0,1:T(2,128)}, u32[]{:S(2)}) copy-start(f32[2,8,96]{2,0,1:T(2,128)} %copy.149) | copy-start | bytes 18436
  165.2 19.5 %copy-start = (f32[8,2,96,2,96,6,1]{2,4,6,5,3,1,0:T(8,128)}, f32[8,2,96,2,96,6,1]{2,4,6,5,3,1,0:T(8,128)S(1)}, u32[]{:S(2)}) copy-start(f32[8,2,96,2,96,6,1]{2,4,6,5,3,1,0:T(8,128)S(1)} %fusion.32) | copy-start | bytes 21233668
  184.8 21.6 %copy-start.13 = (f32[8,2,96]{2,1,0:T(2,128)S(1)}, f32[8,2,96]{2,1,0:T(2,128)}, u32[]{:S(2)}) copy-start(f32[8,2,96]{2,1,0:T(2,128)} %copy.154) | copy-start | bytes 18436
  284.1 198.3 %all-to-all-start.2 = ((bf16[2,96,2,6,768]{4,2,3,0,1:T(2,128)(2,1)}), bf16[2,96,2,6,768]{4,2,3,0,1:T(2,128)(2,1)S(1)}, u32[]{:S(2)}, u32[]{:S(2)}) async-start(bf16[2,96,2,6,768]{4,2,3,0,1:T(2,128)(2,1)} %copy.160), calls=%async_computation.2 | async-start | bytes 7077888 | tf_op jit(solution)/shard_map/all_to_all | solution.py:92
  296.4 177.2 %all-reduce.8.cloned.1.call-start = ((), (), s32[]{:S(2)}) async-start(), calls=%async_computation.3 | async-start | bytes 3145728 | tf_op jit(solution)/shard_map/psum | solution.py:96
Sparse Core Ops, SparseCore 0:
  302.6 170.9 all-reduce.7
where the time goes:
time: 508 us; the launch traced here: 499 us
  matrix products  130 us (26%)
  waiting for transfers between devices  125 us (25%)
  blocking collectives  90.2 us (18%)
  local copies, waits for them, and re-layouts  76 us (15%)
  starting transfers between devices  34.1 us (7%)
  other arithmetic  28.4 us (6%)
  between operations  14.8 us (3%)
    psum x1, blocking collectives, local(): lax.psum((grads[1], grads[2], grads[3], grads[4]), ('batch', 'lat'))  90.2 us
    psum x1, waiting for transfers between devices, local(): lax.psum((grads[1], grads[2], grads[3], grads[4]), ('batch', 'lat'))  70.1 us
    dot_general x3, matrix products, spectral_mix(): jnp.einsum('bmqkni,qnipj->bmpknj', hidden, block_matrix(weight_two), prec...  62.3 us
    dot_general x3, matrix products, spectral_mix(): jnp.einsum('bmqkni,qnipj->bmpknj', mixed, block_matrix(weight_one), preci...  49.8 us
    all_to_all x1, waiting for transfers between devices, local(): lax.all_to_all(spectra, 'lat', split_axis=3, concat_axis=1, tiled=True)  36.7 us
    all_to_all x1, waiting for transfers between devices, local(): lax.all_to_all(spec_cot, 'lat', split_axis=3, concat_axis=1, tiled=True)  18.3 us
    reshape x2, local copies, waits for them, and re-layouts, spectral_mix(): mixed = mixed.reshape(samples, lats, 2, slots, blocks, size)  17.6 us
    all_to_all x1, starting transfers between devices, local(): lax.all_to_all(spec_cot, 'lat', split_axis=3, concat_axis=1, tiled=True)  12.5 us
  transfers between devices with their start and end apart: 4, of which 3 were waited for; matrix products, arithmetic and copies ran while one was open for 12% of the time, Pallas kernels for 0%

commit v1 on v0

v1 whole, which is shorter than its diff:
```python
import functools
import math

import jax
import jax.numpy as jnp
import numpy as np
from jax import lax
from jax.experimental import pallas as pl
from jax.experimental.pallas import tpu as pltpu
from jax.sharding import PartitionSpec as P

MESH = pl.DeviceIdType.MESH
F32, BF16 = jnp.float32, jnp.bfloat16
KP = 96
QUARTER = 24
JB = 8
CHUNKS = QUARTER // JB
HALF = 384
TILES = HALF // 128
LOCAL = 6
SAMPLES = 2
LAT = 96
WIDTH = 180
CH = 768
BS = 96
ROWS = JB * LAT
RB = ROWS // 2
OFFSETS = [(dx, dz, dc) for dx in (1, 0) for dz in (2, 1, 3, 0) for dc in (0, 1)]
WIN = [(0, 512), (0, 768), (256, 768)]
PIECES = [[(0, 0, 96)], [(0, 96, 128), (1, 0, 64)], [(1, 64, 128), (2, 0, 32)], [(2, 32, 128)]]


def lon_tables():
    wpos, kpos = np.arange(WIDTH), np.arange(KP)
    angle = (wpos[:, None] * kpos[None, :] % WIDTH).astype(np.float32) * np.float32(2.0 * math.pi / WIDTH)
    valid = (kpos <= WIDTH // 2).astype(np.float32)[None, :]
    factor = np.float32(1.0 / math.sqrt(WIDTH))
    cosine, sine = np.cos(angle) * valid * factor, np.sin(angle) * valid * factor
    weight = np.where((kpos == 0) | (kpos == WIDTH // 2), 1.0, 2.0).astype(np.float32)[None, :]

    def rows(real, imag):
        both = np.stack([real.T, imag.T]).reshape(2, 4, CHUNKS, JB, WIDTH)
        return both.transpose(1, 2, 0, 3, 4).reshape(2 * KP, WIDTH).astype(BF16)

    return rows(cosine, -sine), rows(cosine * weight, -sine * weight)


def lat_tables():
    pos = np.arange(LAT)
    angle = (pos[:, None] * pos[None, :] % LAT).astype(np.float32) * np.float32(2.0 * math.pi / LAT)
    factor = np.float32(1.0 / math.sqrt(LAT))
    cosine = np.cos(angle) * factor

    def real_form(sign):
        sine = np.sin(angle) * np.float32(factor * sign)
        return np.stack([np.stack([cosine, -sine], -1), np.stack([sine, cosine], -1)], 1).astype(BF16)

    fwd = real_form(-1.0).transpose(1, 0, 3, 2).reshape(2 * LAT, 2 * LAT)
    inv = real_form(1.0).transpose(3, 2, 1, 0).reshape(2 * LAT, 2 * LAT)
    return fwd, inv, np.ascontiguousarray(fwd.T)


def dot(a, b):
    return jnp.dot(a, b, preferred_element_type=F32)


def dot_tb(a, b):
    return lax.dot_general(a, b, (((1,), (1,)), ((), ())), preferred_element_type=F32)


def dot_ta(a, b):
    return lax.dot_general(a, b, (((0,), (0,)), ((), ())), preferred_element_type=F32)


def kernel(
    field, cot, w1, b1, w2, b2, tf, ti, tt, l1, l2, l3,
    out, gout,
    slab, send, recv, gsend, grecv, mixed, hidden, slope, mask, dsec, dfir, scr, bmat, wm, wtmp, bias, acc, gb,
    wraw, braw, slab_sem, out_sem, par_sem, ssem, rsem, own_sem,
):
    batch, me = lax.axis_index("batch"), lax.axis_index("lat")
    half, zz, core = me // 8, (me // 2) % 4, me % 2

    def partner(o):
        dx, dz, dc = o
        return (half + dx) % 2, (zz + dz) % 4, (core + dc) % 2

    def index(part):
        return part[0] * 8 + part[1] * 2 + part[2]

    def source(o):
        dx, dz, dc = o
        return ((half + dx) % 2) * 8 + ((zz + 4 - dz) % 4) * 2 + (core + dc) % 2

    def slab_copy(ref, s, h):
        return pltpu.make_async_copy(ref.at[s, h], slab.at[s * LOCAL + h], slab_sem.at[s * LOCAL + h])

    for s in range(SAMPLES):
        for h in range(LOCAL):
            slab_copy(field, s, h).start()
    params = [
        pltpu.make_async_copy(w1.at[:, pl.ds(half * 4, 4)], wraw.at[0], par_sem.at[0]),
        pltpu.make_async_copy(w2.at[:, pl.ds(half * 4, 4)], wraw.at[1], par_sem.at[1]),
        pltpu.make_async_copy(b1, braw.at[0], par_sem.at[2]),
        pltpu.make_async_copy(b2, braw.at[1], par_sem.at[3]),
    ]
    for copy in params:
        copy.start()

    barrier = pltpu.get_barrier_semaphore()
    for o in OFFSETS:
        if o != (0, 0, 0):
            pl.semaphore_signal(barrier, inc=1, device_id=(batch, index(partner(o))), device_id_type=MESH)

    def lanes(part):
        return pl.ds(pl.multiple_of(part * HALF, 128), HALF)

    def rows16(quarter, jc):
        return pl.ds(pl.multiple_of(quarter * 48 + jc * 16, 16), 16)

    def chunk(jc):
        return pl.ds(pl.multiple_of(jc * 16, 16), 16)

    def inward(a, jc, i):
        to = partner(OFFSETS[i])
        src = send.at[a, to[2], :, rows16(to[1], jc), lanes(to[0])]
        dst = recv.at[a, me, :, chunk(jc), :]
        if OFFSETS[i] == (0, 0, 0):
            return pltpu.make_async_copy(src, dst, own_sem.at[a, jc])
        return pltpu.make_async_remote_copy(
            src, dst, ssem.at[a, jc, i], rsem.at[a, jc, i], device_id=(batch, index(to)), device_id_type=MESH
        )

    def inward_wait(a, jc, i):
        if OFFSETS[i] == (0, 0, 0):
            inward(a, jc, i).wait()
            return
        dst = recv.at[a, source(OFFSETS[i]), :, chunk(jc), :]
        pltpu.make_async_remote_copy(
            dst, dst, ssem.at[a, jc, i], rsem.at[a, jc, i], device_id=(batch, me), device_id_type=MESH
        ).wait_recv()

    def outward(jc, i):
        to = index(partner(OFFSETS[i]))
        src = gsend.at[pl.ds(to * LOCAL, LOCAL), chunk(jc), :]
        dst = grecv.at[core, :, rows16(zz, jc), lanes(half)]
        if OFFSETS[i] == (0, 0, 0):
            return pltpu.make_async_copy(src, dst, own_sem.at[2, jc])
        return pltpu.make_async_remote_copy(
            src, dst, ssem.at[2, jc, i], rsem.at[2, jc, i], device_id=(batch, to), device_id_type=MESH
        )

    def outward_wait(jc, i):
        if OFFSETS[i] == (0, 0, 0):
            outward(jc, i).wait()
            return
        dx, dz, dc = OFFSETS[i]
        fx, fz, fc = (half + dx) % 2, (zz + 4 - dz) % 4, (core + dc) % 2
        dst = grecv.at[fc, :, rows16(fz, jc), lanes(fx)]
        pltpu.make_async_remote_copy(
            dst, dst, ssem.at[2, jc, i], rsem.at[2, jc, i], device_id=(batch, me), device_id_type=MESH
        ).wait_recv()

    def longitude(a, s):
        table = (tf, ti)[a]
        ref = (field, cot)[a]

        def one(h, carry):
            slab_copy(ref, s, h).wait()
            send[a, s, h] = dot(table[...], slab[s * LOCAL + h]).astype(BF16)
            if a == 0:
                slab_copy(cot, s, h).start()
            return carry

        lax.fori_loop(0, LOCAL, one, 0)

    def to_sample(a, jc, s):
        for i, o in enumerate(OFFSETS):

            @pl.when((core + o[2]) % 2 == s)
            def _(i=i):
                inward(a, jc, i).start()

    longitude(0, 0)
    pl.semaphore_wait(barrier, len(OFFSETS) - 1)
    to_sample(0, 0, 0)
    longitude(0, 1)
    to_sample(0, 0, 1)
    for jc in range(1, CHUNKS):
        for i in range(len(OFFSETS)):
            inward(0, jc, i).start()
    longitude(1, 0)
    longitude(1, 1)
    for jc in range(CHUNKS):
        for i in range(len(OFFSETS)):
            inward(1, jc, i).start()

    for copy in params:
        copy.wait()
    row_id = lax.broadcasted_iota(jnp.int32, (BS, HALF), 0)
    col_id = lax.broadcasted_iota(jnp.int32, (BS, HALF), 1)
    for w in range(2):
        for part in range(2):
            total = jnp.zeros((8, HALF), F32)
            for n in range(4):
                place = jnp.where(row_id + n * BS == col_id, 1.0, 0.0).astype(F32)
                placed = dot(wraw[w, part, n].astype(BF16), place.astype(BF16))
                wtmp[part, n * BS : (n + 1) * BS, :] = placed.astype(BF16)
                line = jnp.broadcast_to(braw[w, part, pl.ds(half * 4 + n, 1), :], (8, BS))
                total = total + jnp.dot(line, place, precision=lax.Precision.HIGHEST, preferred_element_type=F32)
            for t in range(TILES):
                c = (2 * t + part) * 128
                bias[w, :, c : c + 128] = total[:, t * 128 : (t + 1) * 128]
        for t in range(TILES):
            for u in range(TILES):
                real = wtmp[0, t * 128 : (t + 1) * 128, u * 128 : (u + 1) * 128]
                imag = wtmp[1, t * 128 : (t + 1) * 128, u * 128 : (u + 1) * 128]
                r, c = t * 256, u * 256
                wm[w, r : r + 128, c : c + 128] = real
                wm[w, r : r + 128, c + 128 : c + 256] = imag
                wm[w, r + 128 : r + 256, c : c + 128] = -imag
                wm[w, r + 128 : r + 256, c + 128 : c + 256] = real
    acc[...] = jnp.zeros_like(acc)
    gb[...] = jnp.zeros_like(gb)

    def gather(a, jc):
        for i in range(len(OFFSETS)):
            inward_wait(a, jc, i)

        def one(l, carry):
            rows = recv[a, l, :, chunk(jc), :].astype(F32).reshape(LOCAL * 16, HALF)
            for t in range(TILES):
                scr[t, pl.ds(pl.multiple_of(l * 96, 8), 96), :] = rows[:, t * 128 : (t + 1) * 128]
            return carry

        lax.fori_loop(0, 16, one, 0)

    def column(j):
        parts = [
            jnp.concatenate([scr[t, pl.ds(q * JB + j, LAT, stride=16), :] for t in range(TILES)], axis=1)
            for q in range(2)
        ]
        return jnp.concatenate(parts, axis=0).astype(BF16)

    def row_block(jc, rb):
        return pl.ds(pl.multiple_of(jc * ROWS + rb * RB, 128), RB)

    def forward(jc, carry):
        gather(0, jc)

        def one(j, c):
            res = dot(l1[...], column(j))
            rows = pl.ds(pl.multiple_of(jc * ROWS + j * LAT, 32), LAT)
            for p in range(2):
                for t in range(TILES):
                    mixed[rows, (2 * t + p) * 128 : (2 * t + p + 1) * 128] = res[
                        p * LAT : (p + 1) * LAT, t * 128 : (t + 1) * 128
                    ].astype(BF16)
            return c

        lax.fori_loop(0, JB, one, 0)

        def mix(rb, c):
            rows = row_block(jc, rb)
            for t in range(TILES):
                lo, hi = WIN[t]
                cols = slice(t * 256, (t + 1) * 256)
                x = dot(mixed[rows, lo:hi], wm[0, lo:hi, cols]) + bias[0, 0:1, cols]
                c0, c1 = math.sqrt(2.0 / math.pi), 0.044715
                xx = x * x
                th = jnp.tanh(x * (c0 + (c0 * c1) * xx))
                gate = 0.5 + 0.5 * th
                hidden[rows, cols] = (x * gate).astype(BF16)
                rise = (0.5 * x) * (1.0 - th * th) * (c0 + (3.0 * c0 * c1) * xx)
                slope[rows, cols] = (gate + rise).astype(BF16)
            for t in range(TILES):
                lo, hi = WIN[t]
                cols = slice(t * 256, (t + 1) * 256)
                y = dot(hidden[rows, lo:hi], wm[1, lo:hi, cols]) + bias[1, 0:1, cols]
                th = jnp.tanh(4.0 * y)
                mask[rows, cols] = (th * th).astype(BF16)
            return c

        lax.fori_loop(0, 2, mix, 0)
        return carry

    lax.fori_loop(0, CHUNKS, forward, 0)

    def backward(jc, carry):
        gather(1, jc)

        def one(j, c):
            res = dot(l2[...], column(j)).astype(BF16)
            rows = pl.ds(pl.multiple_of(jc * ROWS + j * LAT, 32), LAT)
            here = pl.ds(pl.multiple_of(j * LAT, 32), LAT)
            for p in range(2):
                for t in range(TILES):
                    cols = slice((2 * t + p) * 128, (2 * t + p + 1) * 128)
                    part = res[p * LAT : (p + 1) * LAT, t * 128 : (t + 1) * 128].astype(F32)
                    dsec[here, cols] = (part * mask[rows, cols].astype(F32)).astype(BF16)
            return c

        lax.fori_loop(0, JB, one, 0)

        def mix(rb, c):
            rows = row_block(jc, rb)
            here = pl.ds(pl.multiple_of(rb * RB, 128), RB)
            for t in range(TILES):
                lo, hi = WIN[t]
                cols = slice(t * 256, (t + 1) * 256)
                d = dot_tb(dsec[here, lo:hi], wm[1, cols, lo:hi])
                dfir[here, cols] = (d * slope[rows, cols].astype(F32)).astype(BF16)
            for t in range(TILES):
                lo, hi = WIN[t]
                cols = slice(t * 256, (t + 1) * 256)
                d = dot_tb(dfir[here, lo:hi], wm[0, cols, lo:hi]).astype(BF16)
                for jl in range(JB // 2):
                    for p in range(2):
                        bmat[rb * (JB // 2) + jl, p * LAT : (p + 1) * LAT, t * 128 : (t + 1) * 128] = d[
                            jl * LAT : (jl + 1) * LAT, p * 128 : (p + 1) * 128
                        ]
            return c

        lax.fori_loop(0, 2, mix, 0)

        def last(j, c):
            res = dot(l3[...], bmat[j])
            for q in range(2):
                for t in range(TILES):
                    scr[t, pl.ds(q * JB + j, LAT, stride=16), :] = res[
                        q * LAT : (q + 1) * LAT, t * 128 : (t + 1) * 128
                    ]
            return c

        lax.fori_loop(0, JB, last, 0)

        def pack(l, c):
            for t in range(TILES):
                part = scr[t, pl.ds(pl.multiple_of(l * 96, 8), 96), :]
                gsend[pl.ds(l * LOCAL, LOCAL), chunk(jc), t * 128 : (t + 1) * 128] = part.astype(BF16).reshape(
                    LOCAL, 16, 128
                )
            return c

        lax.fori_loop(0, 16, pack, 0)
        for i in range(len(OFFSETS)):
            outward(jc, i).start()

        here = pl.ds(pl.multiple_of(jc * ROWS, 128), ROWS)
        for t in range(TILES):
            lo, hi = WIN[t]
            cols = slice(t * 256, (t + 1) * 256)
            acc[1, cols, lo:hi] += dot_ta(hidden[here, cols], dsec[:, lo:hi])
            acc[0, cols, lo:hi] += dot_ta(mixed[here, cols], dfir[:, lo:hi])
        ones = jnp.ones((16, ROWS), BF16)
        gb[0] += dot(ones, dfir[...])[0:8]
        gb[1] += dot(ones, dsec[...])[0:8]
        return carry

    lax.fori_loop(0, CHUNKS, backward, 0)

    for w in range(2):
        for n in range(4):
            first, last_ = PIECES[n][0][0], PIECES[n][-1][0]
            shift = PIECES[n][0][1]

            def window(get):
                wide = jnp.concatenate([get(first), get(last_)], axis=1)
                return pltpu.roll(wide, (256 - shift) % 256, 1)[:, 0:128]

            for part in range(2):

                def block(u):
                    pieces = []
                    for t, lo, hi in PIECES[n]:
                        r, c = t * 256, u * 256
                        top = acc[w, r + lo : r + hi, c + part * 128 : c + (part + 1) * 128]
                        low = acc[w, r + 128 + lo : r + 128 + hi, c + (1 - part) * 128 : c + (2 - part) * 128]
                        pieces.append(top + low if part == 0 else top - low)
                    return pieces[0] if len(pieces) == 1 else jnp.concatenate(pieces, axis=0)

                b = (w * 2 + part) * 4 + n
                gout[b, 0:BS, :] = window(block)
                gout[b, BS : BS + 8, :] = window(lambda u: gb[w, :, (2 * u + part) * 128 : (2 * u + part + 1) * 128])

    for jc in range(CHUNKS):
        for i in range(len(OFFSETS)):
            outward_wait(jc, i)

    def final(h, carry):
        for s in range(SAMPLES):
            slab[s * LOCAL + h] = dot(tt[...], grecv[s, h]).astype(BF16)
            pltpu.make_async_copy(slab.at[s * LOCAL + h], out.at[s, h], out_sem.at[s * LOCAL + h]).start()
        return carry

    lax.fori_loop(0, LOCAL, final, 0)
    for a in range(3):
        for jc in range(CHUNKS):
            for i, o in enumerate(OFFSETS):
                if o != (0, 0, 0):
                    (outward(jc, i) if a == 2 else inward(a, jc, i)).wait_send()
    for s in range(SAMPLES):
        for h in range(LOCAL):
            pltpu.make_async_copy(slab.at[s * LOCAL + h], out.at[s, h], out_sem.at[s * LOCAL + h]).wait()


def local(field, cotangent, weight_one, bias_one, weight_two, bias_two):
    tf, ti = lon_tables()
    tt = np.ascontiguousarray(tf.T)
    l1, l2, l3 = lat_tables()
    hbm, vmem = pl.BlockSpec(memory_space=pl.ANY), pl.BlockSpec(memory_space=pltpu.VMEM)
    n_off = len(OFFSETS)
    field_grad, blocks = pl.pallas_call(
        kernel,
        name="afno_backward",
        out_shape=(
            jax.ShapeDtypeStruct(field.shape, BF16),
            jax.ShapeDtypeStruct((16, BS + 8, 128), F32),
        ),
        in_specs=[hbm] * 6 + [vmem] * 6,
        out_specs=(hbm, vmem),
        scratch_shapes=[
            pltpu.VMEM((SAMPLES * LOCAL, WIDTH, CH), BF16),
            pltpu.VMEM((2, SAMPLES, LOCAL, 2 * KP, CH), BF16),
            pltpu.VMEM((2, 16, LOCAL, 2 * QUARTER, HALF), BF16),
            pltpu.VMEM((LAT, 2 * QUARTER, HALF), BF16),
            pltpu.VMEM((SAMPLES, LOCAL, 2 * KP, CH), BF16),
            pltpu.VMEM((CHUNKS * ROWS, CH), BF16),
            pltpu.VMEM((CHUNKS * ROWS, CH), BF16),
            pltpu.VMEM((CHUNKS * ROWS, CH), BF16),
            pltpu.VMEM((CHUNKS * ROWS, CH), BF16),
            pltpu.VMEM((ROWS, CH), BF16),
            pltpu.VMEM((ROWS, CH), BF16),
            pltpu.VMEM((TILES, LAT * 16, 128), F32),
            pltpu.VMEM((JB, 2 * LAT, HALF), BF16),
            pltpu.VMEM((2, CH, CH), BF16),
            pltpu.VMEM((2, HALF, HALF), BF16),
            pltpu.VMEM((2, 8, CH), F32),
            pltpu.VMEM((2, CH, CH), F32),
            pltpu.VMEM((2, 8, CH), F32),
            pltpu.VMEM((2, 2, 4, BS, BS), F32),
            pltpu.VMEM((2, 2, 8, BS), F32),
            pltpu.SemaphoreType.DMA((SAMPLES * LOCAL,)),
            pltpu.SemaphoreType.DMA((SAMPLES * LOCAL,)),
            pltpu.SemaphoreType.DMA((4,)),
            pltpu.SemaphoreType.DMA((3, CHUNKS, n_off)),
            pltpu.SemaphoreType.DMA((3, CHUNKS, n_off)),
            pltpu.SemaphoreType.DMA((3, CHUNKS)),
        ],
        compiler_params=pltpu.CompilerParams(
            collective_id=0, has_side_effects=True, vmem_limit_bytes=62 * 1024 * 1024
        ),
        cost_estimate=pl.CostEstimate(flops=10**10, bytes_accessed=10**7, transcendentals=4 * 10**6),
    )(field, cotangent, weight_one, bias_one, weight_two, bias_two, tf, ti, tt, l1, l2, l3)

    half = lax.axis_index("lat") // 8
    spread = jnp.zeros((2,) + blocks.shape, F32)
    spread = lax.dynamic_update_slice(spread, blocks[None], (half, 0, 0, 0))
    total_samples = SAMPLES * lax.axis_size("batch")
    factor = 1.0 / math.sqrt(total_samples * LAT * (WIDTH // 2 + 1))
    total = lax.psum(spread, ("batch", "lat")) * factor
    total = total.reshape(2, 2, 2, 4, BS + 8, 128)[..., :BS].transpose(1, 2, 0, 3, 4, 5).reshape(2, 2, 8, BS + 8, BS)
    return field_grad, total[0, :, :, :BS], total[0, :, :, BS], total[1, :, :, :BS], total[1, :, :, BS]


def solution(mesh):
    in_specs = (P("batch", "lat", None, None), P("batch", "lat", None, None), P(), P(), P(), P())
    out_specs = (P("batch", "lat", None, None), P(), P(), P(), P())
    return jax.shard_map(local, mesh=mesh, in_specs=in_specs, out_specs=out_specs, check_vma=False)
```

time: 508 us -> 311 us (0.61); the launches traced: 499 us -> 311 us
  Pallas kernels: 0 us -> 131 us
  matrix products: 130 us -> 0 us
  blocking collectives: 90.2 us -> 0 us
  local copies, waits for them, and re-layouts: 76 us -> 17.3 us
  starting transfers between devices: 34.1 us -> 0.04 us
  other arithmetic: 28.4 us -> 1.6 us
  waiting for transfers between devices: 125 us -> 147 us
    pallas_call x0 -> x1, Pallas kernels: none -> 131 us  [local(): pl.pallas_call(kernel, name='afno_backward', out_shape=(jax.ShapeDtypeStr...]
    dot_general x12 -> x0, matrix products: 130 us -> none  [the longest x3 62.3 us: spectral_mix(): jnp.einsum('bmqkni,qnipj->bmpknj', hidden, block_matrix(weight_two), prec...]
    psum x1 -> x0, blocking collectives: 90.2 us -> none  [local(): lax.psum((grads[1], grads[2], grads[3], grads[4]), ('batch', 'lat'))]
    psum x1, waiting for transfers between devices: 70.1 us -> 147 us  [local(): total = lax.psum(spread, ('batch', 'lat')) * factor]
    all_to_all x3 -> x0, waiting for transfers between devices: 55 us -> none  [the longest x1 36.7 us: local(): lax.all_to_all(spectra, 'lat', split_axis=3, concat_axis=1, tiled=True)]
    all_to_all x3 -> x0, starting transfers between devices: 34.1 us -> none  [the longest x1 12.5 us: local(): lax.all_to_all(spec_cot, 'lat', split_axis=3, concat_axis=1, tiled=True)]
    reshape x3 -> x0, local copies, waits for them, and re-layouts: 28.1 us -> none  [the longest x2 17.6 us: spectral_mix(): mixed = mixed.reshape(samples, lats, 2, slots, blocks, size)]
    convert_element_type x3 -> x0, local copies, waits for them, and re-layouts: 16.4 us -> none  [the longest x1 5.5 us: spectral_mix(): jnp.einsum('mphq,bhqkc->bmpkc', lat_fwd, spectra, preferred_element_type=...]
  transfers between devices with their start and end apart: 4 -> 1, of which waited for: 3 -> 1; matrix products, arithmetic and copies ran while one was open for 12% -> 2% of each run, Pallas kernels for 0% -> 0%
where the time goes in v1:
time: 311 us
  waiting for transfers between devices  147 us (47%)
  Pallas kernels  131 us (42%)
  local copies, waits for them, and re-layouts  17.3 us (6%)
  between operations  14.1 us (5%)
    psum x1, waiting for transfers between devices, local(): total = lax.psum(spread, ('batch', 'lat')) * factor  147 us
    pallas_call x1, Pallas kernels, local(): pl.pallas_call(kernel, name='afno_backward', out_shape=(jax.ShapeDtypeStr...  131 us
    unnamed x10, local copies, waits for them, and re-layouts  15.2 us
  transfers between devices with their start and end apart: 1, of which 1 were waited for; matrix products, arithmetic and copies ran while one was open for 2% of the time, Pallas kernels for 0%

profile of v1, /device:TPU:1, one launch (start us, length us, event | category | flops | bytes accessed | tf_op | source)
XLA Modules:
  0.0 310.7 jit_solution(14956595525901486752)
XLA Ops:
  7.2 0.0 all-reduce.2.cloned.1.call-start
  7.2 0.0 copy-start.1
  7.2 4.3 %copy.21.field = bf16[2,6,180,768]{3,2,1,0:T(8,128)(2,1)} copy(bf16[2,6,180,768]{3,0,2,1:T(2,128)(2,1)} %param.12) | data formatting | bytes 6635520 | tf_op args[0]
  11.5 0.0 copy-done.1
  11.5 2.2 copy.22.cot
  13.8 131.0 %afno_backward.1 = (bf16[2,6,180,768]{3,2,1,0:T(8,128)(2,1)}, f32[16,104,128]{2,1,0:T(8,128)}) custom-call(bf16[2,6,180,768]{3,2,1,0:T(8,128)(2,1)} %copy.21.field, bf16[2,6,180,768]{3,2,1,0:T(8,128)(2,1)} %copy.22.cot, f32[2,8,96,96]{3,2,1,0:T(8,128)} %w1.1, f32[2,8,96]{2,1,0:T(8,128)} %b1.1, f32[2,8,96,96]{3,2,1,0:T(8,128)} %w2.1, f32[2,8,96]{2,1,0:T(8,128)} %b2.1, ...), custom_call_target="tpu_custom_call" | custom-call | flops 10000000000 | bytes 10000000 | tf_op jit(solution)/shard_map/afno_backward/pallas_call | solution.py:413
  144.7 0.0 copy-start.2
  144.7 0.1 broadcast_in_dim.6
  144.9 1.0 copy-done.2
  145.9 0.1 bitcast_dynamic-update-slice_fusion
  146.0 0.0 copy-start
  146.0 1.3 copy-done
  147.2 0.0 all-reduce.2.cloned.1.call-update
  147.2 6.2 %copy.24 = bf16[2,6,180,768]{3,0,2,1:T(2,128)(2,1)} copy(bf16[2,6,180,768]{3,2,1,0:T(8,128)(2,1)} %get-tuple-element.14) | data formatting | bytes 6635520
  153.5 146.7 %all-reduce.2.cloned.1.call-done = f32[2,16,104,128]{3,2,1,0:T(8,128)} async-done(((f32[2,16,104,128]{3,2,1,0:T(8,128)}), f32[2,16,104,128]{3,2,1,0:T(8,128)}) %all-reduce.2.cloned.1.call-update) | async-done | bytes 1703952 | tf_op jit(solution)/shard_map/psum | solution.py:461
  300.2 1.6 broadcast_multiply_fusion
  301.8 0.1 copy.25
  301.9 1.3 slice_bitcast_fusion
  303.3 0.6 fusion
Async XLA Ops:
  7.2 293.0 %all-reduce.2.cloned.1.call-start = ((), (), s32[]{:S(2)}) async-start(), calls=%async_computation | async-start | bytes 3407872 | tf_op jit(solution)/shard_map/psum | solution.py:461
  7.2 4.3 %copy-start.1 = (bf16[2,6,180,768]{3,0,2,1:T(2,128)(2,1)S(1)}, bf16[2,6,180,768]{3,0,2,1:T(2,128)(2,1)}, u32[]{:S(2)}) copy-start(bf16[2,6,180,768]{3,0,2,1:T(2,128)(2,1)} %param.13) | copy-start | bytes 9953284
  144.7 1.2 copy-start.2
  146.0 1.3 copy-start
Sparse Core Ops, SparseCore 0:
  147.4 152.7 all-reduce.1

commit v2 on v1

--- a/solution.py
+++ b/solution.py
@@ -11,6 +11,8 @@
 
 MESH = pl.DeviceIdType.MESH
 F32, BF16 = jnp.float32, jnp.bfloat16
+BATCH = 8
+UNITS = 5
 KP = 96
 QUARTER = 24
 JB = 8
@@ -74,9 +76,10 @@
 
 def kernel(
     field, cot, w1, b1, w2, b2, tf, ti, tt, l1, l2, l3,
-    out, gout,
+    out, gw1, gb1, gw2, gb2,
     slab, send, recv, gsend, grecv, mixed, hidden, slope, mask, dsec, dfir, scr, bmat, wm, wtmp, bias, acc, gb,
-    wraw, braw, slab_sem, out_sem, par_sem, ssem, rsem, own_sem,
+    wraw, braw, packed, parts, shares, pieces, done, every,
+    slab_sem, out_sem, par_sem, ssem, rsem, own_sem, rs_s, rs_r, sum_s, sum_r, all_s, all_r, ag_s, ag_r,
 ):
     batch, me = lax.axis_index("batch"), lax.axis_index("lat")
     half, zz, core = me // 8, (me // 2) % 4, me % 2
@@ -111,6 +114,8 @@
     for o in OFFSETS:
         if o != (0, 0, 0):
             pl.semaphore_signal(barrier, inc=1, device_id=(batch, index(partner(o))), device_id_type=MESH)
+    for o in range(1, BATCH):
+        pl.semaphore_signal(barrier, inc=1, device_id=((batch + o) % BATCH, me), device_id_type=MESH)
 
     def lanes(part):
         return pl.ds(pl.multiple_of(part * HALF, 128), HALF)
@@ -182,7 +187,7 @@
                 inward(a, jc, i).start()
 
     longitude(0, 0)
-    pl.semaphore_wait(barrier, len(OFFSETS) - 1)
+    pl.semaphore_wait(barrier, len(OFFSETS) - 1 + BATCH - 1)
     to_sample(0, 0, 0)
     longitude(0, 1)
     to_sample(0, 0, 1)
@@ -359,29 +364,117 @@
 
     lax.fori_loop(0, CHUNKS, backward, 0)
 
+    lane = lax.broadcasted_iota(jnp.int32, (BS, 128), 1)
     for w in range(2):
-        for n in range(4):
-            first, last_ = PIECES[n][0][0], PIECES[n][-1][0]
-            shift = PIECES[n][0][1]
-
-            def window(get):
-                wide = jnp.concatenate([get(first), get(last_)], axis=1)
-                return pltpu.roll(wide, (256 - shift) % 256, 1)[:, 0:128]
-
-            for part in range(2):
-
-                def block(u):
-                    pieces = []
-                    for t, lo, hi in PIECES[n]:
-                        r, c = t * 256, u * 256
+        for part in range(2):
+            for t in range(TILES):
+
+                def block(n):
+                    found = []
+                    for u, lo, hi in PIECES[n]:
+                        r, c = u * 256, t * 256
                         top = acc[w, r + lo : r + hi, c + part * 128 : c + (part + 1) * 128]
                         low = acc[w, r + 128 + lo : r + 128 + hi, c + (1 - part) * 128 : c + (2 - part) * 128]
-                        pieces.append(top + low if part == 0 else top - low)
-                    return pieces[0] if len(pieces) == 1 else jnp.concatenate(pieces, axis=0)
-
-                b = (w * 2 + part) * 4 + n
-                gout[b, 0:BS, :] = window(block)
-                gout[b, BS : BS + 8, :] = window(lambda u: gb[w, :, (2 * u + part) * 128 : (2 * u + part + 1) * 128])
+                        found.append(top + low if part == 0 else top - low)
+                    return found[0] if len(found) == 1 else jnp.concatenate(found, axis=0)
+
+                tile = jnp.where(lane < 96 - 32 * t, block(t), block(t + 1)).astype(BF16)
+                for i in range(3):
+                    u = ((w * 2 + part) * TILES + t) * 3 + i
+                    packed[u // UNITS, u % UNITS] = tile[i * 32 : (i + 1) * 32]
+    row = lax.broadcasted_iota(jnp.int32, (32, 128), 0)
+    lines = jnp.zeros((32, 128), F32)
+    for w in range(2):
+        for part in range(2):
+            for t in range(TILES):
+                line = gb[w, 0:1, (2 * t + part) * 128 : (2 * t + part + 1) * 128]
+                lines = jnp.where(row == (w * 2 + part) * TILES + t, jnp.broadcast_to(line, (32, 128)), lines)
+    packed[7, 1] = lines.astype(BF16)
+    for u in range(2, UNITS):
+        packed[7, u] = jnp.zeros((32, 128), BF16)
+
+    def share(o):
+        to = (batch + o) % BATCH
+        return pltpu.make_async_remote_copy(
+            packed.at[to], parts.at[batch], rs_s.at[o], rs_r.at[o], device_id=(to, me), device_id_type=MESH
+        )
+
+    def share_wait(o):
+        dst = parts.at[(batch + BATCH - o) % BATCH]
+        pltpu.make_async_remote_copy(
+            dst, dst, rs_s.at[o], rs_r.at[o], device_id=(batch, me), device_id_type=MESH
+        ).wait_recv()
+
+    for o in range(1, BATCH):
+        share(o).start()
+    parts[batch] = packed[batch]
+    for o in range(1, BATCH):
+        share_wait(o)
+    total = parts[0].astype(F32)
+    for o in range(1, BATCH):
+        total = total + parts[o].astype(F32)
+    shares[...] = total
+
+    mine = me % 8
+
+    def to_reducer(g):
+        return pltpu.make_async_remote_copy(
+            shares.at[g], pieces.at[mine], sum_s.at[g], sum_r.at[mine],
+            device_id=(batch, half * 8 + g), device_id_type=MESH,
+        )
+
+    def to_all(i):
+        return pltpu.make_async_remote_copy(
+            done.at[half, mine], done.at[half, mine], all_s.at[i], all_r.at[half, mine],
+            device_id=(batch, index(partner(OFFSETS[i]))), device_id_type=MESH,
+        )
+
+    for g in range(UNITS):
+
+        @pl.when(mine != g)
+        def _(g=g):
+            to_reducer(g).start()
+
+    @pl.when(mine < UNITS)
+    def _():
+        pieces[mine] = shares[mine]
+        for g in range(8):
+
+            @pl.when(mine != g)
+            def _(g=g):
+                dst = pieces.at[g]
+                pltpu.make_async_remote_copy(
+                    dst, dst, sum_s.at[0], sum_r.at[g], device_id=(batch, me), device_id_type=MESH
+                ).wait_recv()
+
+        whole = pieces[0]
+        for g in range(1, 8):
+            whole = whole + pieces[g]
+        samples = SAMPLES * BATCH
+        done[half, mine] = (whole * (1.0 / math.sqrt(samples * LAT * (WIDTH // 2 + 1)))).astype(BF16)
+        for i, o in enumerate(OFFSETS):
+            if o != (0, 0, 0):
+                to_all(i).start()
+
+    for hf in range(2):
+        for g in range(UNITS):
+
+            @pl.when(me != hf * 8 + g)
+            def _(hf=hf, g=g):
+                dst = done.at[hf, g]
+                pltpu.make_async_remote_copy(
+                    dst, dst, all_s.at[0], all_r.at[hf, g], device_id=(batch, me), device_id_type=MESH
+                ).wait_recv()
+
+    def gathered(o):
+        to = (batch + o) % BATCH
+        return pltpu.make_async_remote_copy(
+            done, every.at[batch], ag_s.at[o], ag_r.at[o], device_id=(to, me), device_id_type=MESH
+        )
+
+    for o in range(1, BATCH):
+        gathered(o).start()
+    every[batch] = done[...]
 
     for jc in range(CHUNKS):
         for i in range(len(OFFSETS)):
@@ -394,6 +487,48 @@
         return carry
 
     lax.fori_loop(0, LOCAL, final, 0)
+
+    for o in range(1, BATCH):
+        dst = every.at[(batch + BATCH - o) % BATCH]
+        pltpu.make_async_remote_copy(
+            dst, dst, ag_s.at[o], ag_r.at[o], device_id=(batch, me), device_id_type=MESH
+        ).wait_recv()
+    for w, gw, gbias in ((0, gw1, gb1), (1, gw2, gb2)):
+        for part in range(2):
+            for hf in range(2):
+                tiles, lines = [], []
+                for t in range(TILES):
+                    k = (w * 2 + part) * TILES + t
+                    found = [every[u // UNITS, hf, u % UNITS] for u in range(3 * k, 3 * k + 3)]
+                    tiles.append(jnp.concatenate(found, axis=0).astype(F32))
+                    lines.append(jnp.broadcast_to(every[7, hf, 1].astype(F32)[k : k + 1], (8, 128)))
+
+                def blocks(x, n):
+                    if n == 0:
+                        return x[0][:, :BS]
+                    if n == 3:
+                        return pltpu.roll(x[2], BS, 1)[:, :BS]
+                    return pltpu.roll(jnp.concatenate(x[n - 1 : n + 1], axis=1), 128 + 32 * n, 1)[:, :BS]
+
+                for n in range(4):
+                    gw[part, hf * 4 + n] = blocks(tiles, n)
+                    gbias[part, hf * 4 + n : hf * 4 + n + 1, :] = blocks(lines, n)[0:1]
+
+    for o in range(1, BATCH):
+        share(o).wait_send()
+        gathered(o).wait_send()
+    for g in range(UNITS):
+
+        @pl.when(mine != g)
+        def _(g=g):
+            to_reducer(g).wait_send()
+
+    @pl.when(mine < UNITS)
+    def _():
+        for i, o in enumerate(OFFSETS):
+            if o != (0, 0, 0):
+                to_all(i).wait_send()
+
     for a in range(3):
         for jc in range(CHUNKS):
             for i, o in enumerate(OFFSETS):
@@ -410,15 +545,18 @@
     l1, l2, l3 = lat_tables()
     hbm, vmem = pl.BlockSpec(memory_space=pl.ANY), pl.BlockSpec(memory_space=pltpu.VMEM)
     n_off = len(OFFSETS)
-    field_grad, blocks = pl.pallas_call(
+    return pl.pallas_call(
         kernel,
         name="afno_backward",
         out_shape=(
             jax.ShapeDtypeStruct(field.shape, BF16),
-            jax.ShapeDtypeStruct((16, BS + 8, 128), F32),
+            jax.ShapeDtypeStruct(weight_one.shape, F32),
+            jax.ShapeDtypeStruct(bias_one.shape, F32),
+            jax.ShapeDtypeStruct(weight_two.shape, F32),
+            jax.ShapeDtypeStruct(bias_two.shape, F32),
         ),
         in_specs=[hbm] * 6 + [vmem] * 6,
-        out_specs=(hbm, vmem),
+        out_specs=(hbm, vmem, vmem, vmem, vmem),
         scratch_shapes=[
             pltpu.VMEM((SAMPLES * LOCAL, WIDTH, CH), BF16),
             pltpu.VMEM((2, SAMPLES, LOCAL, 2 * KP, CH), BF16),
@@ -440,12 +578,26 @@
             pltpu.VMEM((2, 8, CH), F32),
             pltpu.VMEM((2, 2, 4, BS, BS), F32),
             pltpu.VMEM((2, 2, 8, BS), F32),
+            pltpu.VMEM((BATCH, UNITS, 32, 128), BF16),
+            pltpu.VMEM((BATCH, UNITS, 32, 128), BF16),
+            pltpu.VMEM((UNITS, 32, 128), F32),
+            pltpu.VMEM((8, 32, 128), F32),
+            pltpu.VMEM((2, UNITS, 32, 128), BF16),
+            pltpu.VMEM((BATCH, 2, UNITS, 32, 128), BF16),
             pltpu.SemaphoreType.DMA((SAMPLES * LOCAL,)),
             pltpu.SemaphoreType.DMA((SAMPLES * LOCAL,)),
             pltpu.SemaphoreType.DMA((4,)),
             pltpu.SemaphoreType.DMA((3, CHUNKS, n_off)),
             pltpu.SemaphoreType.DMA((3, CHUNKS, n_off)),
             pltpu.SemaphoreType.DMA((3, CHUNKS)),
+            pltpu.SemaphoreType.DMA((BATCH,)),
+            pltpu.SemaphoreType.DMA((BATCH,)),
+            pltpu.SemaphoreType.DMA((UNITS,)),
+            pltpu.SemaphoreType.DMA((8,)),
+            pltpu.SemaphoreType.DMA((n_off,)),
+            pltpu.SemaphoreType.DMA((2, UNITS)),
+            pltpu.SemaphoreType.DMA((BATCH,)),
+            pltpu.SemaphoreType.DMA((BATCH,)),
         ],
         compiler_params=pltpu.CompilerParams(
             collective_id=0, has_side_effects=True, vmem_limit_bytes=62 * 1024 * 1024
@@ -453,15 +605,6 @@
         cost_estimate=pl.CostEstimate(flops=10**10, bytes_accessed=10**7, transcendentals=4 * 10**6),
     )(field, cotangent, weight_one, bias_one, weight_two, bias_two, tf, ti, tt, l1, l2, l3)
 
-    half = lax.axis_index("lat") // 8
-    spread = jnp.zeros((2,) + blocks.shape, F32)
-    spread = lax.dynamic_update_slice(spread, blocks[None], (half, 0, 0, 0))
-    total_samples = SAMPLES * lax.axis_size("batch")
-    factor = 1.0 / math.sqrt(total_samples * LAT * (WIDTH // 2 + 1))
-    total = lax.psum(spread, ("batch", "lat")) * factor
-    total = total.reshape(2, 2, 2, 4, BS + 8, 128)[..., :BS].transpose(1, 2, 0, 3, 4, 5).reshape(2, 2, 8, BS + 8, BS)
-    return field_grad, total[0, :, :, :BS], total[0, :, :, BS], total[1, :, :, :BS], total[1, :, :, BS]
-
 
 def solution(mesh):
     in_specs = (P("batch", "lat", None, None), P("batch", "lat", None, None), P(), P(), P(), P())

time: 311 us -> 173 us (0.56)
  waiting for transfers between devices: 147 us -> 0 us
  Pallas kernels: 131 us -> 156 us
  between operations: 14.1 us -> 0.68 us
    psum x1 -> x0, waiting for transfers between devices: 147 us -> none  [local(): total = lax.psum(spread, ('batch', 'lat')) * factor]
    pallas_call x1, Pallas kernels: 131 us -> 156 us  [local(): pl.pallas_call(kernel, name='afno_backward', out_shape=(jax.ShapeDtypeStr...]
    pallas_call x0 -> x1, local copies, waits for them, and re-layouts: none -> 6.35 us  [local(): pl.pallas_call(kernel, name='afno_backward', out_shape=(jax.ShapeDtypeStr...]
    unnamed x10 -> x16, local copies, waits for them, and re-layouts: 15.2 us -> 9.42 us
  transfers between devices with their start and end apart: 1 -> 0, of which waited for: 1 -> 0; matrix products, arithmetic and copies ran while one was open for 2% -> 0% of each run, Pallas kernels for 0% -> 0%
where the time goes in v2:
time: 173 us
  Pallas kernels  156 us (90%)
  local copies, waits for them, and re-layouts  15.8 us (9%)
    pallas_call x1, Pallas kernels, local(): pl.pallas_call(kernel, name='afno_backward', out_shape=(jax.ShapeDtypeStr...  156 us
    unnamed x16, local copies, waits for them, and re-layouts  9.42 us
    pallas_call x1, local copies, waits for them, and re-layouts, local(): pl.pallas_call(kernel, name='afno_backward', out_shape=(jax.ShapeDtypeStr...  6.35 us

profile of v2, /device:TPU:1, one launch (start us, length us, event | category | flops | bytes accessed | tf_op | source)
XLA Modules:
  0.0 172.8 jit_solution(1514417242027221603)
XLA Ops:
  0.6 0.0 copy-start
  0.6 4.3 %copy.17.field = bf16[2,6,180,768]{3,2,1,0:T(8,128)(2,1)} copy(bf16[2,6,180,768]{3,0,2,1:T(2,128)(2,1)} %param.12) | data formatting | bytes 6635520 | tf_op args[0]
  4.9 0.0 copy-done
  4.9 2.2 %copy.18.cot = bf16[2,6,180,768]{3,2,1,0:T(8,128)(2,1)} copy(bf16[2,6,180,768]{3,0,2,1:T(2,128)(2,1)S(1)} %copy-done) | data formatting | bytes 6635520 | tf_op args[1]
  7.1 156.3 %afno_backward.1 = (bf16[2,6,180,768]{3,2,1,0:T(8,128)(2,1)}, f32[2,8,96,96]{3,2,1,0:T(8,128)}, f32[2,8,96]{2,1,0:T(8,128)}, f32[2,8,96,96]{3,2,1,0:T(8,128)}, f32[2,8,96]{2,1,0:T(8,128)}) custom-call(bf16[2,6,180,768]{3,2,1,0:T(8,128)(2,1)} %copy.17.field, bf16[2,6,180,768]{3,2,1,0:T(8,128)(2,1)} %copy.18.cot, f32[2,8,96,96]{3,2,1,0:T(8,128)} %w1.1, ...), custom_call_target="tpu_custom_call" | custom-call | flops 10000000000 | bytes 10000000 | tf_op jit(solution)/shard_map/afno_backward/pallas_call | solution.py:548
  163.4 0.0 copy-start.2
  163.5 0.0 copy-start.4
  163.5 0.0 copy-start.1
  163.5 0.0 copy-start.3
  163.5 6.3 %copy.19 = bf16[2,6,180,768]{3,0,2,1:T(2,128)(2,1)} copy(bf16[2,6,180,768]{3,2,1,0:T(8,128)(2,1)} %get-tuple-element.5) | data formatting | bytes 6635520 | tf_op jit(solution)/shard_map/afno_backward/pallas_call | solution.py:548
  169.8 0.0 copy-done.2
  169.8 0.9 copy.24
  170.7 0.0 copy-done.4
  170.7 0.6 copy.25
  171.3 0.0 copy-done.1
  171.3 0.9 copy.26
  172.2 0.0 copy-done.3
  172.2 0.6 copy.27
Async XLA Ops:
  0.6 4.3 %copy-start = (bf16[2,6,180,768]{3,0,2,1:T(2,128)(2,1)S(1)}, bf16[2,6,180,768]{3,0,2,1:T(2,128)(2,1)}, u32[]{:S(2)}) copy-start(bf16[2,6,180,768]{3,0,2,1:T(2,128)(2,1)} %param.13) | copy-start | bytes 9953284
  163.4 6.4 %copy-start.2 = (f32[2,8,96,96]{3,2,1,0:T(8,128)S(1)}, f32[2,8,96,96]{3,2,1,0:T(8,128)}, u32[]{:S(2)}) copy-start(f32[2,8,96,96]{3,2,1,0:T(8,128)} %get-tuple-element.16) | copy-start | bytes 1769476
  163.5 7.3 %copy-start.4 = (f32[2,8,96]{2,1,0:T(8,128)S(1)}, f32[2,8,96]{2,1,0:T(8,128)}, u32[]{:S(2)}) copy-start(f32[2,8,96]{2,1,0:T(8,128)} %get-tuple-element.17) | copy-start | bytes 18436
  163.5 7.9 %copy-start.1 = (f32[2,8,96,96]{3,2,1,0:T(8,128)S(1)}, f32[2,8,96,96]{3,2,1,0:T(8,128)}, u32[]{:S(2)}) copy-start(f32[2,8,96,96]{3,2,1,0:T(8,128)} %get-tuple-element.18) | copy-start | bytes 1769476
  163.5 8.7 %copy-start.3 = (f32[2,8,96]{2,1,0:T(8,128)S(1)}, f32[2,8,96]{2,1,0:T(8,128)}, u32[]{:S(2)}) copy-start(f32[2,8,96]{2,1,0:T(8,128)} %get-tuple-element.19) | copy-start | bytes 18436

commit v3 on v2

--- a/solution.py
+++ b/solution.py
@@ -11,7 +11,8 @@
 
 MESH = pl.DeviceIdType.MESH
 F32, BF16 = jnp.float32, jnp.bfloat16
-BATCH = 8
+NY = 4
+BATCH = 2 * NY
 UNITS = 5
 KP = 96
 QUARTER = 24
@@ -27,7 +28,8 @@
 BS = 96
 ROWS = JB * LAT
 RB = ROWS // 2
-OFFSETS = [(dx, dz, dc) for dx in (1, 0) for dz in (2, 1, 3, 0) for dc in (0, 1)]
+OFFSETS = [(dx, dz, dc) for dz in (1, 3, 2, 0) for dx in (1, 0) for dc in (1, 0)]
+CUTS = (10, 20, 26)
 WIN = [(0, 512), (0, 768), (256, 768)]
 PIECES = [[(0, 0, 96)], [(0, 96, 128), (1, 0, 64)], [(1, 64, 128), (2, 0, 32)], [(2, 32, 128)]]
 
@@ -44,7 +46,13 @@
         both = np.stack([real.T, imag.T]).reshape(2, 4, CHUNKS, JB, WIDTH)
         return both.transpose(1, 2, 0, 3, 4).reshape(2 * KP, WIDTH).astype(BF16)
 
-    return rows(cosine, -sine), rows(cosine * weight, -sine * weight)
+    def paired(table):
+        both = np.zeros((SAMPLES, 2 * KP, WIDTH, SAMPLES), BF16)
+        for s in range(SAMPLES):
+            both[s, :, :, s] = table
+        return both.reshape(SAMPLES * 2 * KP, WIDTH * SAMPLES)
+
+    return paired(rows(cosine, -sine)), paired(rows(cosine * weight, -sine * weight))
 
 
 def lat_tables():
@@ -75,14 +83,19 @@
 
 
 def kernel(
-    field, cot, w1, b1, w2, b2, tf, ti, tt, l1, l2, l3,
-    out, gw1, gb1, gw2, gb2,
-    slab, send, recv, gsend, grecv, mixed, hidden, slope, mask, dsec, dfir, scr, bmat, wm, wtmp, bias, acc, gb,
-    wraw, braw, packed, parts, shares, pieces, done, every,
-    slab_sem, out_sem, par_sem, ssem, rsem, own_sem, rs_s, rs_r, sum_s, sum_r, all_s, all_r, ag_s, ag_r,
+    field, cot, w1, b1, w2, b2, tf_hbm, ti_hbm, l1_hbm, l2_hbm, l3_hbm,
+    grecv, every,
+    slab, send, recv, gsend, mixed, hidden, slope, mask, dsec, dfir, scr, bmat, wm, wtmp, bias, acc, gb,
+    wraw, braw, packed, parts, shares, pieces, done, tf, ti, l1, l2, l3,
+    table_sem, slab_sem, every_sem, par_sem, ssem, rsem, own_sem, rs_s, rs_r, sum_s, sum_r, all_s, all_r, ag_s, ag_r,
 ):
     batch, me = lax.axis_index("batch"), lax.axis_index("lat")
     half, zz, core = me // 8, (me // 2) % 4, me % 2
+    side, yy = batch // NY, batch % NY
+    other = (1 - side) * NY + yy
+
+    def along(o):
+        return side * NY + (yy + o) % NY
 
     def partner(o):
         dx, dz, dc = o
@@ -95,12 +108,18 @@
         dx, dz, dc = o
         return ((half + dx) % 2) * 8 + ((zz + 4 - dz) % 4) * 2 + (core + dc) % 2
 
-    def slab_copy(ref, s, h):
-        return pltpu.make_async_copy(ref.at[s, h], slab.at[s * LOCAL + h], slab_sem.at[s * LOCAL + h])
-
-    for s in range(SAMPLES):
-        for h in range(LOCAL):
-            slab_copy(field, s, h).start()
+    def slab_copy(a, h):
+        return pltpu.make_async_copy((field, cot)[a].at[h], slab.at[a, h], slab_sem.at[a, h])
+
+    tables = [
+        pltpu.make_async_copy(src, dst, table_sem.at[i])
+        for i, (src, dst) in enumerate(((tf_hbm, tf), (ti_hbm, ti), (l1_hbm, l1), (l2_hbm, l2), (l3_hbm, l3)))
+    ]
+    tables[0].start()
+    for h in range(LOCAL):
+        slab_copy(0, h).start()
+    for copy in tables[1:]:
+        copy.start()
     params = [
         pltpu.make_async_copy(w1.at[:, pl.ds(half * 4, 4)], wraw.at[0], par_sem.at[0]),
         pltpu.make_async_copy(w2.at[:, pl.ds(half * 4, 4)], wraw.at[1], par_sem.at[1]),
@@ -114,21 +133,23 @@
     for o in OFFSETS:
         if o != (0, 0, 0):
             pl.semaphore_signal(barrier, inc=1, device_id=(batch, index(partner(o))), device_id_type=MESH)
-    for o in range(1, BATCH):
-        pl.semaphore_signal(barrier, inc=1, device_id=((batch + o) % BATCH, me), device_id_type=MESH)
+        pl.semaphore_signal(barrier, inc=1, device_id=(other, index(partner(o))), device_id_type=MESH)
+    for o in range(1, NY):
+        for to in (along(o), (1 - side) * NY + (yy + o) % NY):
+            pl.semaphore_signal(barrier, inc=1, device_id=(to, me), device_id_type=MESH)
 
     def lanes(part):
         return pl.ds(pl.multiple_of(part * HALF, 128), HALF)
 
-    def rows16(quarter, jc):
-        return pl.ds(pl.multiple_of(quarter * 48 + jc * 16, 16), 16)
+    def rows16(sample, quarter, jc):
+        return pl.ds(pl.multiple_of(sample * 2 * KP + quarter * 48 + jc * 16, 16), 16)
 
     def chunk(jc):
         return pl.ds(pl.multiple_of(jc * 16, 16), 16)
 
     def inward(a, jc, i):
         to = partner(OFFSETS[i])
-        src = send.at[a, to[2], :, rows16(to[1], jc), lanes(to[0])]
+        src = send.at[a, :, rows16(to[2], to[1], jc), lanes(to[0])]
         dst = recv.at[a, me, :, chunk(jc), :]
         if OFFSETS[i] == (0, 0, 0):
             return pltpu.make_async_copy(src, dst, own_sem.at[a, jc])
@@ -148,7 +169,7 @@
     def outward(jc, i):
         to = index(partner(OFFSETS[i]))
         src = gsend.at[pl.ds(to * LOCAL, LOCAL), chunk(jc), :]
-        dst = grecv.at[core, :, rows16(zz, jc), lanes(half)]
+        dst = grecv.at[:, rows16(core, zz, jc), lanes(half)]
         if OFFSETS[i] == (0, 0, 0):
             return pltpu.make_async_copy(src, dst, own_sem.at[2, jc])
         return pltpu.make_async_remote_copy(
@@ -161,46 +182,37 @@
             return
         dx, dz, dc = OFFSETS[i]
         fx, fz, fc = (half + dx) % 2, (zz + 4 - dz) % 4, (core + dc) % 2
-        dst = grecv.at[fc, :, rows16(fz, jc), lanes(fx)]
+        dst = grecv.at[:, rows16(fc, fz, jc), lanes(fx)]
         pltpu.make_async_remote_copy(
             dst, dst, ssem.at[2, jc, i], rsem.at[2, jc, i], device_id=(batch, me), device_id_type=MESH
         ).wait_recv()
 
-    def longitude(a, s):
+    def longitude(a):
         table = (tf, ti)[a]
-        ref = (field, cot)[a]
 
         def one(h, carry):
-            slab_copy(ref, s, h).wait()
-            send[a, s, h] = dot(table[...], slab[s * LOCAL + h]).astype(BF16)
+            slab_copy(a, h).wait()
             if a == 0:
-                slab_copy(cot, s, h).start()
+                slab_copy(1, h).start()
+            pair = slab[a, h].reshape(WIDTH * SAMPLES, CH)
+            send[a, h] = dot(table[...], pair).astype(BF16)
             return carry
 
         lax.fori_loop(0, LOCAL, one, 0)
 
-    def to_sample(a, jc, s):
-        for i, o in enumerate(OFFSETS):
-
-            @pl.when((core + o[2]) % 2 == s)
-            def _(i=i):
-                inward(a, jc, i).start()
-
-    longitude(0, 0)
-    pl.semaphore_wait(barrier, len(OFFSETS) - 1 + BATCH - 1)
-    to_sample(0, 0, 0)
-    longitude(0, 1)
-    to_sample(0, 0, 1)
-    for jc in range(1, CHUNKS):
+    tables[0].wait()
+    longitude(0)
+    pl.semaphore_wait(barrier, 2 * len(OFFSETS) - 1 + 2 * (NY - 1))
+    for jc in range(CHUNKS):
         for i in range(len(OFFSETS)):
             inward(0, jc, i).start()
-    longitude(1, 0)
-    longitude(1, 1)
+    tables[1].wait()
+    longitude(1)
     for jc in range(CHUNKS):
         for i in range(len(OFFSETS)):
             inward(1, jc, i).start()
 
-    for copy in params:
+    for copy in params + tables[2:]:
         copy.wait()
     row_id = lax.broadcasted_iota(jnp.int32, (BS, HALF), 0)
     col_id = lax.broadcasted_iota(jnp.int32, (BS, HALF), 1)
@@ -348,8 +360,11 @@
             return c
 
         lax.fori_loop(0, 16, pack, 0)
-        for i in range(len(OFFSETS)):
-            outward(jc, i).start()
+
+        @pl.when(jc < 1)
+        def _():
+            for i in range(len(OFFSETS)):
+                outward(jc, i).start()
 
         here = pl.ds(pl.multiple_of(jc * ROWS, 128), ROWS)
         for t in range(TILES):
@@ -394,26 +409,26 @@
         packed[7, u] = jnp.zeros((32, 128), BF16)
 
     def share(o):
-        to = (batch + o) % BATCH
         return pltpu.make_async_remote_copy(
-            packed.at[to], parts.at[batch], rs_s.at[o], rs_r.at[o], device_id=(to, me), device_id_type=MESH
+            packed.at[(batch + o) % BATCH], parts.at[batch], rs_s.at[o], rs_r.at[o],
+            device_id=((batch + o) % BATCH, me), device_id_type=MESH,
         )
 
-    def share_wait(o):
+    for o in range(1, BATCH):
+        share(o).start()
+    back = [(jc, i) for jc in range(1, CHUNKS) for i in range(len(OFFSETS))]
+    for jc, i in back[:CUTS[0]]:
+        outward(jc, i).start()
+    parts[batch] = packed[batch]
+    for o in range(1, BATCH):
         dst = parts.at[(batch + BATCH - o) % BATCH]
         pltpu.make_async_remote_copy(
             dst, dst, rs_s.at[o], rs_r.at[o], device_id=(batch, me), device_id_type=MESH
         ).wait_recv()
-
-    for o in range(1, BATCH):
-        share(o).start()
-    parts[batch] = packed[batch]
-    for o in range(1, BATCH):
-        share_wait(o)
     total = parts[0].astype(F32)
     for o in range(1, BATCH):
         total = total + parts[o].astype(F32)
-    shares[...] = total
+    shares[...] = total.astype(BF16)
 
     mine = me % 8
 
@@ -423,17 +438,21 @@
             device_id=(batch, half * 8 + g), device_id_type=MESH,
         )
 
-    def to_all(i):
+    def to_all(i, far):
         return pltpu.make_async_remote_copy(
-            done.at[half, mine], done.at[half, mine], all_s.at[i], all_r.at[half, mine],
-            device_id=(batch, index(partner(OFFSETS[i]))), device_id_type=MESH,
+            done.at[side, half, mine], done.at[side, half, mine], all_s.at[i, far], all_r.at[side, half, mine],
+            device_id=((batch, other)[far], index(partner(OFFSETS[i]))), device_id_type=MESH,
         )
 
+    listeners = [(i, far) for i, o in enumerate(OFFSETS) for far in range(2) if (o, far) != ((0, 0, 0), 0)]
     for g in range(UNITS):
 
         @pl.when(mine != g)
         def _(g=g):
             to_reducer(g).start()
+
+    for jc, i in back[CUTS[0] : CUTS[1]]:
+        outward(jc, i).start()
 
     @pl.when(mine < UNITS)
     def _():
@@ -447,61 +466,91 @@
                     dst, dst, sum_s.at[0], sum_r.at[g], device_id=(batch, me), device_id_type=MESH
                 ).wait_recv()
 
-        whole = pieces[0]
+        whole = pieces[0].astype(F32)
         for g in range(1, 8):
-            whole = whole + pieces[g]
-        samples = SAMPLES * BATCH
-        done[half, mine] = (whole * (1.0 / math.sqrt(samples * LAT * (WIDTH // 2 + 1)))).astype(BF16)
-        for i, o in enumerate(OFFSETS):
-            if o != (0, 0, 0):
-                to_all(i).start()
-
-    for hf in range(2):
-        for g in range(UNITS):
-
-            @pl.when(me != hf * 8 + g)
-            def _(hf=hf, g=g):
-                dst = done.at[hf, g]
-                pltpu.make_async_remote_copy(
-                    dst, dst, all_s.at[0], all_r.at[hf, g], device_id=(batch, me), device_id_type=MESH
-                ).wait_recv()
+            whole = whole + pieces[g].astype(F32)
+        samples = SAMPLES * 2 * NY
+        done[side, half, mine] = (whole * (1.0 / math.sqrt(samples * LAT * (WIDTH // 2 + 1)))).astype(BF16)
+        for i, far in listeners:
+            to_all(i, far).start()
+
+    for jc, i in back[CUTS[1] : CUTS[2]]:
+        outward(jc, i).start()
+
+    for sd in range(2):
+        for hf in range(2):
+            for g in range(UNITS):
+
+                @pl.when((side != sd) | (half != hf) | (mine != g))
+                def _(sd=sd, hf=hf, g=g):
+                    dst = done.at[sd, hf, g]
+                    pltpu.make_async_remote_copy(
+                        dst, dst, all_s.at[0, 0], all_r.at[sd, hf, g], device_id=(batch, me), device_id_type=MESH
+                    ).wait_recv()
 
     def gathered(o):
-        to = (batch + o) % BATCH
         return pltpu.make_async_remote_copy(
-            done, every.at[batch], ag_s.at[o], ag_r.at[o], device_id=(to, me), device_id_type=MESH
+            done, every.at[yy], ag_s.at[o], ag_r.at[o], device_id=(along(o), me), device_id_type=MESH
         )
 
-    for o in range(1, BATCH):
+    for o in range(1, NY):
         gathered(o).start()
-    every[batch] = done[...]
+    kept = pltpu.make_async_copy(done, every.at[yy], every_sem)
+    kept.start()
+    for jc, i in back[CUTS[2] :]:
+        outward(jc, i).start()
 
     for jc in range(CHUNKS):
         for i in range(len(OFFSETS)):
             outward_wait(jc, i)
-
-    def final(h, carry):
-        for s in range(SAMPLES):
-            slab[s * LOCAL + h] = dot(tt[...], grecv[s, h]).astype(BF16)
-            pltpu.make_async_copy(slab.at[s * LOCAL + h], out.at[s, h], out_sem.at[s * LOCAL + h]).start()
-        return carry
-
-    lax.fori_loop(0, LOCAL, final, 0)
-
-    for o in range(1, BATCH):
-        dst = every.at[(batch + BATCH - o) % BATCH]
+    for o in range(1, NY):
+        dst = every.at[(yy + NY - o) % NY]
         pltpu.make_async_remote_copy(
             dst, dst, ag_s.at[o], ag_r.at[o], device_id=(batch, me), device_id_type=MESH
         ).wait_recv()
+    kept.wait()
+
+    for o in range(1, BATCH):
+        share(o).wait_send()
+    for o in range(1, NY):
+        gathered(o).wait_send()
+    for g in range(UNITS):
+
+        @pl.when(mine != g)
+        def _(g=g):
+            to_reducer(g).wait_send()
+
+    @pl.when(mine < UNITS)
+    def _():
+        for i, far in listeners:
+            to_all(i, far).wait_send()
+
+    for a in range(3):
+        for jc in range(CHUNKS):
+            for i, o in enumerate(OFFSETS):
+                if o != (0, 0, 0):
+                    (outward(jc, i) if a == 2 else inward(a, jc, i)).wait_send()
+
+
+def finish(
+    every, grecv, tt, out, gw1_hbm, gb1_hbm, gw2_hbm, gb2_hbm,
+    slab, pair, sums, table, gw1, gb1, gw2, gb2, in_sem, out_sem, par_sem,
+):
+    fetch = [pltpu.make_async_copy(tt, table, par_sem.at[0]), pltpu.make_async_copy(every, sums, par_sem.at[1])]
+    fetch[1].start()
+    fetch[0].start()
+    for h in range(LOCAL):
+        pltpu.make_async_copy(grecv.at[h], slab.at[h], in_sem.at[h]).start()
+    fetch[1].wait()
     for w, gw, gbias in ((0, gw1, gb1), (1, gw2, gb2)):
         for part in range(2):
             for hf in range(2):
                 tiles, lines = [], []
                 for t in range(TILES):
                     k = (w * 2 + part) * TILES + t
-                    found = [every[u // UNITS, hf, u % UNITS] for u in range(3 * k, 3 * k + 3)]
+                    found = [sums[u // UNITS % NY, u // UNITS // NY, hf, u % UNITS] for u in range(3 * k, 3 * k + 3)]
                     tiles.append(jnp.concatenate(found, axis=0).astype(F32))
-                    lines.append(jnp.broadcast_to(every[7, hf, 1].astype(F32)[k : k + 1], (8, 128)))
+                    lines.append(jnp.broadcast_to(sums[3, 1, hf, 1].astype(F32)[k : k + 1], (8, 128)))
 
                 def blocks(x, n):
                     if n == 0:
@@ -513,56 +562,51 @@
                 for n in range(4):
                     gw[part, hf * 4 + n] = blocks(tiles, n)
                     gbias[part, hf * 4 + n : hf * 4 + n + 1, :] = blocks(lines, n)[0:1]
-
-    for o in range(1, BATCH):
-        share(o).wait_send()
-        gathered(o).wait_send()
-    for g in range(UNITS):
-
-        @pl.when(mine != g)
-        def _(g=g):
-            to_reducer(g).wait_send()
-
-    @pl.when(mine < UNITS)
-    def _():
-        for i, o in enumerate(OFFSETS):
-            if o != (0, 0, 0):
-                to_all(i).wait_send()
-
-    for a in range(3):
-        for jc in range(CHUNKS):
-            for i, o in enumerate(OFFSETS):
-                if o != (0, 0, 0):
-                    (outward(jc, i) if a == 2 else inward(a, jc, i)).wait_send()
-    for s in range(SAMPLES):
-        for h in range(LOCAL):
-            pltpu.make_async_copy(slab.at[s * LOCAL + h], out.at[s, h], out_sem.at[s * LOCAL + h]).wait()
+    outs = [
+        pltpu.make_async_copy(src, dst, par_sem.at[2 + i])
+        for i, (src, dst) in enumerate(((gw1, gw1_hbm), (gb1, gb1_hbm), (gw2, gw2_hbm), (gb2, gb2_hbm)))
+    ]
+    for copy in outs:
+        copy.start()
+    fetch[0].wait()
+
+    def one(h, carry):
+        pltpu.make_async_copy(grecv.at[h], slab.at[h], in_sem.at[h]).wait()
+        pair[h] = dot(table[...], slab[h]).astype(BF16).reshape(WIDTH, SAMPLES, CH)
+        pltpu.make_async_copy(pair.at[h], out.at[h], out_sem.at[h]).start()
+        return carry
+
+    lax.fori_loop(0, LOCAL, one, 0)
+    for copy in outs:
+        copy.wait()
+    for h in range(LOCAL):
+        pltpu.make_async_copy(pair.at[h], out.at[h], out_sem.at[h]).wait()
 
 
 def local(field, cotangent, weight_one, bias_one, weight_two, bias_two):
     tf, ti = lon_tables()
     tt = np.ascontiguousarray(tf.T)
     l1, l2, l3 = lat_tables()
-    hbm, vmem = pl.BlockSpec(memory_space=pl.ANY), pl.BlockSpec(memory_space=pltpu.VMEM)
+    hbm = pl.BlockSpec(memory_space=pl.ANY)
     n_off = len(OFFSETS)
-    return pl.pallas_call(
+
+    def pairs(x):
+        return x.transpose(1, 2, 0, 3)
+
+    grecv, every = pl.pallas_call(
         kernel,
         name="afno_backward",
         out_shape=(
-            jax.ShapeDtypeStruct(field.shape, BF16),
-            jax.ShapeDtypeStruct(weight_one.shape, F32),
-            jax.ShapeDtypeStruct(bias_one.shape, F32),
-            jax.ShapeDtypeStruct(weight_two.shape, F32),
-            jax.ShapeDtypeStruct(bias_two.shape, F32),
+            jax.ShapeDtypeStruct((LOCAL, SAMPLES * 2 * KP, CH), BF16),
+            jax.ShapeDtypeStruct((NY, 2, 2, UNITS, 32, 128), BF16),
         ),
-        in_specs=[hbm] * 6 + [vmem] * 6,
-        out_specs=(hbm, vmem, vmem, vmem, vmem),
+        in_specs=[hbm] * 11,
+        out_specs=(hbm, hbm),
         scratch_shapes=[
-            pltpu.VMEM((SAMPLES * LOCAL, WIDTH, CH), BF16),
-            pltpu.VMEM((2, SAMPLES, LOCAL, 2 * KP, CH), BF16),
+            pltpu.VMEM((2, LOCAL, WIDTH, SAMPLES, CH), BF16),
+            pltpu.VMEM((2, LOCAL, SAMPLES * 2 * KP, CH), BF16),
             pltpu.VMEM((2, 16, LOCAL, 2 * QUARTER, HALF), BF16),
             pltpu.VMEM((LAT, 2 * QUARTER, HALF), BF16),
-            pltpu.VMEM((SAMPLES, LOCAL, 2 * KP, CH), BF16),
             pltpu.VMEM((CHUNKS * ROWS, CH), BF16),
             pltpu.VMEM((CHUNKS * ROWS, CH), BF16),
             pltpu.VMEM((CHUNKS * ROWS, CH), BF16),
@@ -580,12 +624,17 @@
             pltpu.VMEM((2, 2, 8, BS), F32),
             pltpu.VMEM((BATCH, UNITS, 32, 128), BF16),
             pltpu.VMEM((BATCH, UNITS, 32, 128), BF16),
-            pltpu.VMEM((UNITS, 32, 128), F32),
-            pltpu.VMEM((8, 32, 128), F32),
-            pltpu.VMEM((2, UNITS, 32, 128), BF16),
-            pltpu.VMEM((BATCH, 2, UNITS, 32, 128), BF16),
-            pltpu.SemaphoreType.DMA((SAMPLES * LOCAL,)),
-            pltpu.SemaphoreType.DMA((SAMPLES * LOCAL,)),
+            pltpu.VMEM((UNITS, 32, 128), BF16),
+            pltpu.VMEM((8, 32, 128), BF16),
+            pltpu.VMEM((2, 2, UNITS, 32, 128), BF16),
+            pltpu.VMEM(tf.shape, BF16),
+            pltpu.VMEM(ti.shape, BF16),
+            pltpu.VMEM(l1.shape, BF16),
+            pltpu.VMEM(l2.shape, BF16),
+            pltpu.VMEM(l3.shape, BF16),
+            pltpu.SemaphoreType.DMA((5,)),
+            pltpu.SemaphoreType.DMA((2, LOCAL)),
+            pltpu.SemaphoreType.DMA,
             pltpu.SemaphoreType.DMA((4,)),
             pltpu.SemaphoreType.DMA((3, CHUNKS, n_off)),
             pltpu.SemaphoreType.DMA((3, CHUNKS, n_off)),
@@ -594,16 +643,47 @@
             pltpu.SemaphoreType.DMA((BATCH,)),
             pltpu.SemaphoreType.DMA((UNITS,)),
             pltpu.SemaphoreType.DMA((8,)),
-            pltpu.SemaphoreType.DMA((n_off,)),
-            pltpu.SemaphoreType.DMA((2, UNITS)),
-            pltpu.SemaphoreType.DMA((BATCH,)),
-            pltpu.SemaphoreType.DMA((BATCH,)),
+            pltpu.SemaphoreType.DMA((n_off, 2)),
+            pltpu.SemaphoreType.DMA((2, 2, UNITS)),
+            pltpu.SemaphoreType.DMA((NY,)),
+            pltpu.SemaphoreType.DMA((NY,)),
         ],
         compiler_params=pltpu.CompilerParams(
             collective_id=0, has_side_effects=True, vmem_limit_bytes=62 * 1024 * 1024
         ),
         cost_estimate=pl.CostEstimate(flops=10**10, bytes_accessed=10**7, transcendentals=4 * 10**6),
-    )(field, cotangent, weight_one, bias_one, weight_two, bias_two, tf, ti, tt, l1, l2, l3)
+    )(pairs(field), pairs(cotangent), weight_one, bias_one, weight_two, bias_two, tf, ti, l1, l2, l3)
+
+    wshape, bshape = weight_one.shape, bias_one.shape
+    field_grad, *rest = pl.pallas_call(
+        finish,
+        name="finish",
+        out_shape=(
+            jax.ShapeDtypeStruct((LOCAL, WIDTH, SAMPLES, CH), BF16),
+            jax.ShapeDtypeStruct(wshape, F32),
+            jax.ShapeDtypeStruct(bshape, F32),
+            jax.ShapeDtypeStruct(wshape, F32),
+            jax.ShapeDtypeStruct(bshape, F32),
+        ),
+        in_specs=[hbm] * 3,
+        out_specs=[hbm] * 5,
+        scratch_shapes=[
+            pltpu.VMEM(grecv.shape, BF16),
+            pltpu.VMEM((LOCAL, WIDTH, SAMPLES, CH), BF16),
+            pltpu.VMEM(every.shape, BF16),
+            pltpu.VMEM(tt.shape, BF16),
+            pltpu.VMEM(wshape, F32),
+            pltpu.VMEM(bshape, F32),
+            pltpu.VMEM(wshape, F32),
+            pltpu.VMEM(bshape, F32),
+            pltpu.SemaphoreType.DMA((LOCAL,)),
+            pltpu.SemaphoreType.DMA((LOCAL,)),
+            pltpu.SemaphoreType.DMA((6,)),
+        ],
+        compiler_params=pltpu.CompilerParams(vmem_limit_bytes=62 * 1024 * 1024),
+        cost_estimate=pl.CostEstimate(flops=2 * 10**9, bytes_accessed=8 * 10**6, transcendentals=0),
+    )(every, grecv, tt)
+    return (field_grad.transpose(2, 0, 1, 3), *rest)
 
 
 def solution(mesh):

time: 173 us -> 145 us (0.84)
  local copies, waits for them, and re-layouts: 15.8 us -> 0 us
  Pallas kernels: 156 us -> 144 us
    pallas_call x1, Pallas kernels: 156 us -> 138 us  [local(): pl.pallas_call(kernel, name='afno_backward', out_shape=(jax.ShapeDtypeStr...]
    unnamed x16 -> x0, local copies, waits for them, and re-layouts: 9.42 us -> none
    pallas_call x1 -> x0, local copies, waits for them, and re-layouts: 6.35 us -> none  [local(): pl.pallas_call(kernel, name='afno_backward', out_shape=(jax.ShapeDtypeStr...]
    pallas_call x0 -> x1, Pallas kernels: none -> 5.99 us  [local(): pl.pallas_call(finish, name='finish', out_shape=(jax.ShapeDtypeStruct((LO...]
where the time goes in v3:
time: 145 us
  Pallas kernels  144 us (99%)
    pallas_call x1, Pallas kernels, local(): pl.pallas_call(kernel, name='afno_backward', out_shape=(jax.ShapeDtypeStr...  138 us
    pallas_call x1, Pallas kernels, local(): pl.pallas_call(finish, name='finish', out_shape=(jax.ShapeDtypeStruct((LO...  5.99 us

profile of v3, /device:TPU:1, one launch (start us, length us, event | category | flops | bytes accessed | tf_op | source)
XLA Modules:
  0.0 144.7 jit_solution(3249411843245912332)
XLA Ops:
  0.6 138.1 %afno_backward.1 = (bf16[6,384,768]{2,1,0:T(8,128)(2,1)}, bf16[4,2,2,5,32,128]{5,4,3,2,1,0:T(8,128)(2,1)}) custom-call(bf16[6,180,2,768]{3,2,1,0:T(2,128)(2,1)} %bitcast.3, bf16[6,180,2,768]{3,2,1,0:T(2,128)(2,1)} %bitcast.4, f32[2,8,96,96]{3,2,1,0:T(8,128)} %w1.1, f32[2,8,96]{2,1,0:T(8,128)} %b1.1, f32[2,8,96,96]{3,2,1,0:T(8,128)} %w2.1, f32[2,8,96]{2,1,0:T(8,128)} %b2.1, ...), custom_call_target="tpu_custom_call" | custom-call | flops 10000000000 | bytes 10000000 | tf_op jit(solution)/shard_map/afno_backward/pallas_call | solution.py:596
  138.7 6.0 %finish.1 = (bf16[6,180,2,768]{3,2,1,0:T(2,128)(2,1)}, f32[2,8,96,96]{3,2,1,0:T(8,128)}, f32[2,8,96]{2,1,0:T(8,128)}, f32[2,8,96,96]{3,2,1,0:T(8,128)}, f32[2,8,96]{2,1,0:T(8,128)}) custom-call(bf16[4,2,2,5,32,128]{5,4,3,2,1,0:T(8,128)(2,1)} %get-tuple-element.12.every, bf16[6,384,768]{2,1,0:T(8,128)(2,1)} %get-tuple-element.13.grecv, ...), custom_call_target="tpu_custom_call" | custom-call | flops 2000000000 | bytes 8000000 | tf_op jit(solution)/shard_map/finish/pallas_call | solution.py:658

commit v4 on v3

--- a/solution.py
+++ b/solution.py
@@ -29,7 +29,7 @@
 ROWS = JB * LAT
 RB = ROWS // 2
 OFFSETS = [(dx, dz, dc) for dz in (1, 3, 2, 0) for dx in (1, 0) for dc in (1, 0)]
-CUTS = (10, 20, 26)
+CUTS = (12, 20, 26)
 WIN = [(0, 512), (0, 768), (256, 768)]
 PIECES = [[(0, 0, 96)], [(0, 96, 128), (1, 0, 64)], [(1, 64, 128), (2, 0, 32)], [(2, 32, 128)]]
 
@@ -87,7 +87,7 @@
     grecv, every,
     slab, send, recv, gsend, mixed, hidden, slope, mask, dsec, dfir, scr, bmat, wm, wtmp, bias, acc, gb,
     wraw, braw, packed, parts, shares, pieces, done, tf, ti, l1, l2, l3,
-    table_sem, slab_sem, every_sem, par_sem, ssem, rsem, own_sem, rs_s, rs_r, sum_s, sum_r, all_s, all_r, ag_s, ag_r,
+    table_sem, slab_sem, every_sem, par_sem, ssem, rsem, own_sem, rs_s, rs_r, sum_s, sum_r, all_s, all_r, ag_s, ag_r, pass_s, pass_r, early_s, early_r,
 ):
     batch, me = lax.axis_index("batch"), lax.axis_index("lat")
     half, zz, core = me // 8, (me // 2) % 4, me % 2
@@ -147,6 +147,29 @@
     def chunk(jc):
         return pl.ds(pl.multiple_of(jc * 16, 16), 16)
 
+    def early(part, i):
+        to = partner(OFFSETS[i])
+        here = pl.ds(part * (LOCAL // 2), LOCAL // 2)
+        src = send.at[0, here, rows16(to[2], to[1], 0), lanes(to[0])]
+        dst = recv.at[0, me, here, chunk(0), :]
+        if OFFSETS[i] == (0, 0, 0):
+            return pltpu.make_async_copy(src, dst, early_s.at[i + part])
+        sems = (early_s.at[i], early_r.at[i]) if part == 0 else (ssem.at[0, 0, i], rsem.at[0, 0, i])
+        return pltpu.make_async_remote_copy(
+            src, dst, *sems, device_id=(batch, index(to)), device_id_type=MESH
+        )
+
+    def early_wait(i):
+        for part in range(2):
+            if OFFSETS[i] == (0, 0, 0):
+                early(part, i).wait()
+                continue
+            dst = recv.at[0, source(OFFSETS[i]), pl.ds(part * (LOCAL // 2), LOCAL // 2), chunk(0), :]
+            sems = (early_s.at[i], early_r.at[i]) if part == 0 else (ssem.at[0, 0, i], rsem.at[0, 0, i])
+            pltpu.make_async_remote_copy(
+                dst, dst, *sems, device_id=(batch, me), device_id_type=MESH
+            ).wait_recv()
+
     def inward(a, jc, i):
         to = partner(OFFSETS[i])
         src = send.at[a, :, rows16(to[2], to[1], jc), lanes(to[0])]
@@ -187,7 +210,7 @@
             dst, dst, ssem.at[2, jc, i], rsem.at[2, jc, i], device_id=(batch, me), device_id_type=MESH
         ).wait_recv()
 
-    def longitude(a):
+    def longitude(a, first=0, last=LOCAL):
         table = (tf, ti)[a]
 
         def one(h, carry):
@@ -198,12 +221,17 @@
             send[a, h] = dot(table[...], pair).astype(BF16)
             return carry
 
-        lax.fori_loop(0, LOCAL, one, 0)
+        lax.fori_loop(first, last, one, 0)
 
     tables[0].wait()
-    longitude(0)
+    longitude(0, 0, LOCAL // 2)
     pl.semaphore_wait(barrier, 2 * len(OFFSETS) - 1 + 2 * (NY - 1))
-    for jc in range(CHUNKS):
+    for i in range(len(OFFSETS)):
+        early(0, i).start()
+    longitude(0, LOCAL // 2, LOCAL)
+    for i in range(len(OFFSETS)):
+        early(1, i).start()
+    for jc in range(1, CHUNKS):
         for i in range(len(OFFSETS)):
             inward(0, jc, i).start()
     tables[1].wait()
@@ -241,8 +269,21 @@
     gb[...] = jnp.zeros_like(gb)
 
     def gather(a, jc):
-        for i in range(len(OFFSETS)):
-            inward_wait(a, jc, i)
+        if a == 0:
+
+            @pl.when(jc == 0)
+            def _():
+                for i in range(len(OFFSETS)):
+                    early_wait(i)
+
+            @pl.when(jc > 0)
+            def _():
+                for i in range(len(OFFSETS)):
+                    inward_wait(a, jc, i)
+
+        else:
+            for i in range(len(OFFSETS)):
+                inward_wait(a, jc, i)
 
         def one(l, carry):
             rows = recv[a, l, :, chunk(jc), :].astype(F32).reshape(LOCAL * 16, HALF)
@@ -303,7 +344,7 @@
 
     lax.fori_loop(0, CHUNKS, forward, 0)
 
-    def backward(jc, carry):
+    def to_hidden(jc):
         gather(1, jc)
 
         def one(j, c):
@@ -327,6 +368,13 @@
                 cols = slice(t * 256, (t + 1) * 256)
                 d = dot_tb(dsec[here, lo:hi], wm[1, cols, lo:hi])
                 dfir[here, cols] = (d * slope[rows, cols].astype(F32)).astype(BF16)
+            return c
+
+        lax.fori_loop(0, 2, mix, 0)
+
+    def to_spectra(jc):
+        def mix(rb, c):
+            here = pl.ds(pl.multiple_of(rb * RB, 128), RB)
             for t in range(TILES):
                 lo, hi = WIN[t]
                 cols = slice(t * 256, (t + 1) * 256)
@@ -361,11 +409,7 @@
 
         lax.fori_loop(0, 16, pack, 0)
 
-        @pl.when(jc < 1)
-        def _():
-            for i in range(len(OFFSETS)):
-                outward(jc, i).start()
-
+    def to_weights(jc):
         here = pl.ds(pl.multiple_of(jc * ROWS, 128), ROWS)
         for t in range(TILES):
             lo, hi = WIN[t]
@@ -375,9 +419,22 @@
         ones = jnp.ones((16, ROWS), BF16)
         gb[0] += dot(ones, dfir[...])[0:8]
         gb[1] += dot(ones, dsec[...])[0:8]
+
+    def backward(jc, carry):
+        to_hidden(jc)
+        to_spectra(jc)
+
+        @pl.when(jc < 1)
+        def _():
+            for i in range(len(OFFSETS)):
+                outward(jc, i).start()
+
+        to_weights(jc)
         return carry
 
-    lax.fori_loop(0, CHUNKS, backward, 0)
+    lax.fori_loop(0, CHUNKS - 1, backward, 0)
+    to_hidden(CHUNKS - 1)
+    to_weights(CHUNKS - 1)
 
     lane = lax.broadcasted_iota(jnp.int32, (BS, 128), 1)
     for w in range(2):
@@ -419,6 +476,7 @@
     back = [(jc, i) for jc in range(1, CHUNKS) for i in range(len(OFFSETS))]
     for jc, i in back[:CUTS[0]]:
         outward(jc, i).start()
+    to_spectra(CHUNKS - 1)
     parts[batch] = packed[batch]
     for o in range(1, BATCH):
         dst = parts.at[(batch + BATCH - o) % BATCH]
@@ -490,7 +548,14 @@
 
     def gathered(o):
         return pltpu.make_async_remote_copy(
-            done, every.at[yy], ag_s.at[o], ag_r.at[o], device_id=(along(o), me), device_id_type=MESH
+            done.at[core], every.at[yy, core], ag_s.at[o], ag_r.at[o],
+            device_id=(along(o), me), device_id_type=MESH,
+        )
+
+    def passed(o):
+        got = every.at[(yy + NY - o) % NY, core]
+        return pltpu.make_async_remote_copy(
+            got, got, pass_s.at[o], pass_r.at[o], device_id=(batch, me + 1 - 2 * core), device_id_type=MESH
         )
 
     for o in range(1, NY):
@@ -500,13 +565,19 @@
     for jc, i in back[CUTS[2] :]:
         outward(jc, i).start()
 
+    for o in range(1, NY):
+        dst = every.at[(yy + NY - o) % NY, core]
+        pltpu.make_async_remote_copy(
+            dst, dst, ag_s.at[o], ag_r.at[o], device_id=(batch, me), device_id_type=MESH
+        ).wait_recv()
+        passed(o).start()
     for jc in range(CHUNKS):
         for i in range(len(OFFSETS)):
             outward_wait(jc, i)
     for o in range(1, NY):
-        dst = every.at[(yy + NY - o) % NY]
+        dst = every.at[(yy + NY - o) % NY, 1 - core]
         pltpu.make_async_remote_copy(
-            dst, dst, ag_s.at[o], ag_r.at[o], device_id=(batch, me), device_id_type=MESH
+            dst, dst, pass_s.at[o], pass_r.at[o], device_id=(batch, me), device_id_type=MESH
         ).wait_recv()
     kept.wait()
 
@@ -514,6 +585,7 @@
         share(o).wait_send()
     for o in range(1, NY):
         gathered(o).wait_send()
+        passed(o).wait_send()
     for g in range(UNITS):
 
         @pl.when(mine != g)
@@ -528,7 +600,10 @@
     for a in range(3):
         for jc in range(CHUNKS):
             for i, o in enumerate(OFFSETS):
-                if o != (0, 0, 0):
+                if o != (0, 0, 0) and (a, jc) == (0, 0):
+                    early(0, i).wait_send()
+                    early(1, i).wait_send()
+                elif o != (0, 0, 0):
                     (outward(jc, i) if a == 2 else inward(a, jc, i)).wait_send()
 
 
@@ -647,6 +722,10 @@
             pltpu.SemaphoreType.DMA((2, 2, UNITS)),
             pltpu.SemaphoreType.DMA((NY,)),
             pltpu.SemaphoreType.DMA((NY,)),
+            pltpu.SemaphoreType.DMA((NY,)),
+            pltpu.SemaphoreType.DMA((NY,)),
+            pltpu.SemaphoreType.DMA((n_off + 1,)),
+            pltpu.SemaphoreType.DMA((n_off,)),
         ],
         compiler_params=pltpu.CompilerParams(
             collective_id=0, has_side_effects=True, vmem_limit_bytes=62 * 1024 * 1024

time: 145 us -> 142 us (0.979)
  Pallas kernels: 144 us -> 141 us
    pallas_call x1, Pallas kernels: 138 us -> 135 us  [local(): pl.pallas_call(kernel, name='afno_backward', out_shape=(jax.ShapeDtypeStr...]
where the time goes in v4:
time: 142 us
  Pallas kernels  141 us (99%)
    pallas_call x1, Pallas kernels, local(): pl.pallas_call(kernel, name='afno_backward', out_shape=(jax.ShapeDtypeStr...  135 us
    pallas_call x1, Pallas kernels, local(): pl.pallas_call(finish, name='finish', out_shape=(jax.ShapeDtypeStruct((LO...  5.99 us

profile of v4, /device:TPU:1, one launch (start us, length us, event | category | flops | bytes accessed | tf_op | source)
XLA Modules:
  0.0 141.8 jit_solution(3338851362229617808)
XLA Ops:
  0.6 135.1 %afno_backward.1 = (bf16[6,384,768]{2,1,0:T(8,128)(2,1)}, bf16[4,2,2,5,32,128]{5,4,3,2,1,0:T(8,128)(2,1)}) custom-call(bf16[6,180,2,768]{3,2,1,0:T(2,128)(2,1)} %bitcast.3, bf16[6,180,2,768]{3,2,1,0:T(2,128)(2,1)} %bitcast.4, f32[2,8,96,96]{3,2,1,0:T(8,128)} %w1.1, f32[2,8,96]{2,1,0:T(8,128)} %b1.1, f32[2,8,96,96]{3,2,1,0:T(8,128)} %w2.1, f32[2,8,96]{2,1,0:T(8,128)} %b2.1, ...), custom_call_target="tpu_custom_call" | custom-call | flops 10000000000 | bytes 10000000 | tf_op jit(solution)/shard_map/afno_backward/pallas_call | solution.py:671
  135.8 6.0 %finish.1 = (bf16[6,180,2,768]{3,2,1,0:T(2,128)(2,1)}, f32[2,8,96,96]{3,2,1,0:T(8,128)}, f32[2,8,96]{2,1,0:T(8,128)}, f32[2,8,96,96]{3,2,1,0:T(8,128)}, f32[2,8,96]{2,1,0:T(8,128)}) custom-call(bf16[4,2,2,5,32,128]{5,4,3,2,1,0:T(8,128)(2,1)} %get-tuple-element.12.every, bf16[6,384,768]{2,1,0:T(8,128)(2,1)} %get-tuple-element.13.grecv, ...), custom_call_target="tpu_custom_call" | custom-call | flops 2000000000 | bytes 8000000 | tf_op jit(solution)/shard_map/finish/pallas_call | solution.py:737

commit v5 on v4

--- a/solution.py
+++ b/solution.py
@@ -87,7 +87,7 @@
     grecv, every,
     slab, send, recv, gsend, mixed, hidden, slope, mask, dsec, dfir, scr, bmat, wm, wtmp, bias, acc, gb,
     wraw, braw, packed, parts, shares, pieces, done, tf, ti, l1, l2, l3,
-    table_sem, slab_sem, every_sem, par_sem, ssem, rsem, own_sem, rs_s, rs_r, sum_s, sum_r, all_s, all_r, ag_s, ag_r, pass_s, pass_r, early_s, early_r,
+    table_sem, slab_sem, every_sem, par_sem, ssem, rsem, rs_s, rs_r, sum_s, sum_r, all_s, all_r, ag_s, ag_r, pass_s, pass_r,
 ):
     batch, me = lax.axis_index("batch"), lax.axis_index("lat")
     half, zz, core = me // 8, (me // 2) % 4, me % 2
@@ -103,10 +103,6 @@
 
     def index(part):
         return part[0] * 8 + part[1] * 2 + part[2]
-
-    def source(o):
-        dx, dz, dc = o
-        return ((half + dx) % 2) * 8 + ((zz + 4 - dz) % 4) * 2 + (core + dc) % 2
 
     def slab_copy(a, h):
         return pltpu.make_async_copy((field, cot)[a].at[h], slab.at[a, h], slab_sem.at[a, h])
@@ -153,62 +149,41 @@
         src = send.at[0, here, rows16(to[2], to[1], 0), lanes(to[0])]
         dst = recv.at[0, me, here, chunk(0), :]
         if OFFSETS[i] == (0, 0, 0):
-            return pltpu.make_async_copy(src, dst, early_s.at[i + part])
-        sems = (early_s.at[i], early_r.at[i]) if part == 0 else (ssem.at[0, 0, i], rsem.at[0, 0, i])
+            return pltpu.make_async_copy(src, dst, rsem.at[0, 0])
         return pltpu.make_async_remote_copy(
-            src, dst, *sems, device_id=(batch, index(to)), device_id_type=MESH
+            src, dst, ssem.at[0, 0], rsem.at[0, 0], device_id=(batch, index(to)), device_id_type=MESH
         )
-
-    def early_wait(i):
-        for part in range(2):
-            if OFFSETS[i] == (0, 0, 0):
-                early(part, i).wait()
-                continue
-            dst = recv.at[0, source(OFFSETS[i]), pl.ds(part * (LOCAL // 2), LOCAL // 2), chunk(0), :]
-            sems = (early_s.at[i], early_r.at[i]) if part == 0 else (ssem.at[0, 0, i], rsem.at[0, 0, i])
-            pltpu.make_async_remote_copy(
-                dst, dst, *sems, device_id=(batch, me), device_id_type=MESH
-            ).wait_recv()
 
     def inward(a, jc, i):
         to = partner(OFFSETS[i])
         src = send.at[a, :, rows16(to[2], to[1], jc), lanes(to[0])]
         dst = recv.at[a, me, :, chunk(jc), :]
         if OFFSETS[i] == (0, 0, 0):
-            return pltpu.make_async_copy(src, dst, own_sem.at[a, jc])
+            return pltpu.make_async_copy(src, dst, rsem.at[a, jc])
         return pltpu.make_async_remote_copy(
-            src, dst, ssem.at[a, jc, i], rsem.at[a, jc, i], device_id=(batch, index(to)), device_id_type=MESH
+            src, dst, ssem.at[a, jc], rsem.at[a, jc], device_id=(batch, index(to)), device_id_type=MESH
         )
 
-    def inward_wait(a, jc, i):
-        if OFFSETS[i] == (0, 0, 0):
-            inward(a, jc, i).wait()
-            return
-        dst = recv.at[a, source(OFFSETS[i]), :, chunk(jc), :]
+    def arrived(a, jc, region):
         pltpu.make_async_remote_copy(
-            dst, dst, ssem.at[a, jc, i], rsem.at[a, jc, i], device_id=(batch, me), device_id_type=MESH
+            region, region, ssem.at[a, jc], rsem.at[a, jc], device_id=(batch, me), device_id_type=MESH
         ).wait_recv()
+
+    def left(a, jc):
+        region = recv.at[0, pl.ds(0, len(OFFSETS) - 1), :, pl.ds(0, 16), :]
+        pltpu.make_async_remote_copy(
+            region, region, ssem.at[a, jc], rsem.at[a, jc], device_id=(batch, me), device_id_type=MESH
+        ).wait_send()
 
     def outward(jc, i):
         to = index(partner(OFFSETS[i]))
         src = gsend.at[pl.ds(to * LOCAL, LOCAL), chunk(jc), :]
         dst = grecv.at[:, rows16(core, zz, jc), lanes(half)]
         if OFFSETS[i] == (0, 0, 0):
-            return pltpu.make_async_copy(src, dst, own_sem.at[2, jc])
+            return pltpu.make_async_copy(src, dst, rsem.at[2, jc])
         return pltpu.make_async_remote_copy(
-            src, dst, ssem.at[2, jc, i], rsem.at[2, jc, i], device_id=(batch, to), device_id_type=MESH
+            src, dst, ssem.at[2, jc], rsem.at[2, jc], device_id=(batch, to), device_id_type=MESH
         )
-
-    def outward_wait(jc, i):
-        if OFFSETS[i] == (0, 0, 0):
-            outward(jc, i).wait()
-            return
-        dx, dz, dc = OFFSETS[i]
-        fx, fz, fc = (half + dx) % 2, (zz + 4 - dz) % 4, (core + dc) % 2
-        dst = grecv.at[:, rows16(fc, fz, jc), lanes(fx)]
-        pltpu.make_async_remote_copy(
-            dst, dst, ssem.at[2, jc, i], rsem.at[2, jc, i], device_id=(batch, me), device_id_type=MESH
-        ).wait_recv()
 
     def longitude(a, first=0, last=LOCAL):
         table = (tf, ti)[a]
@@ -269,21 +244,7 @@
     gb[...] = jnp.zeros_like(gb)
 
     def gather(a, jc):
-        if a == 0:
-
-            @pl.when(jc == 0)
-            def _():
-                for i in range(len(OFFSETS)):
-                    early_wait(i)
-
-            @pl.when(jc > 0)
-            def _():
-                for i in range(len(OFFSETS)):
-                    inward_wait(a, jc, i)
-
-        else:
-            for i in range(len(OFFSETS)):
-                inward_wait(a, jc, i)
+        arrived(a, jc, recv.at[a, :, :, chunk(jc), :])
 
         def one(l, carry):
             rows = recv[a, l, :, chunk(jc), :].astype(F32).reshape(LOCAL * 16, HALF)
@@ -572,8 +533,7 @@
         ).wait_recv()
         passed(o).start()
     for jc in range(CHUNKS):
-        for i in range(len(OFFSETS)):
-            outward_wait(jc, i)
+        arrived(2, jc, grecv.at[:, pl.ds(0, 128), :])
     for o in range(1, NY):
         dst = every.at[(yy + NY - o) % NY, 1 - core]
         pltpu.make_async_remote_copy(
@@ -599,12 +559,7 @@
 
     for a in range(3):
         for jc in range(CHUNKS):
-            for i, o in enumerate(OFFSETS):
-                if o != (0, 0, 0) and (a, jc) == (0, 0):
-                    early(0, i).wait_send()
-                    early(1, i).wait_send()
-                elif o != (0, 0, 0):
-                    (outward(jc, i) if a == 2 else inward(a, jc, i)).wait_send()
+            left(a, jc)
 
 
 def finish(
@@ -688,7 +643,7 @@
             pltpu.VMEM((CHUNKS * ROWS, CH), BF16),
             pltpu.VMEM((ROWS, CH), BF16),
             pltpu.VMEM((ROWS, CH), BF16),
-            pltpu.VMEM((TILES, LAT * 16, 128), F32),
+            pltpu.VMEM((TILES, LAT * 16 + 16, 128), F32),
             pltpu.VMEM((JB, 2 * LAT, HALF), BF16),
             pltpu.VMEM((2, CH, CH), BF16),
             pltpu.VMEM((2, HALF, HALF), BF16),
@@ -711,8 +666,7 @@
             pltpu.SemaphoreType.DMA((2, LOCAL)),
             pltpu.SemaphoreType.DMA,
             pltpu.SemaphoreType.DMA((4,)),
-            pltpu.SemaphoreType.DMA((3, CHUNKS, n_off)),
-            pltpu.SemaphoreType.DMA((3, CHUNKS, n_off)),
+            pltpu.SemaphoreType.DMA((3, CHUNKS)),
             pltpu.SemaphoreType.DMA((3, CHUNKS)),
             pltpu.SemaphoreType.DMA((BATCH,)),
             pltpu.SemaphoreType.DMA((BATCH,)),
@@ -724,8 +678,6 @@
             pltpu.SemaphoreType.DMA((NY,)),
             pltpu.SemaphoreType.DMA((NY,)),
             pltpu.SemaphoreType.DMA((NY,)),
-            pltpu.SemaphoreType.DMA((n_off + 1,)),
-            pltpu.SemaphoreType.DMA((n_off,)),
         ],
         compiler_params=pltpu.CompilerParams(
             collective_id=0, has_side_effects=True, vmem_limit_bytes=62 * 1024 * 1024

time: 142 us -> 139 us (0.979)
  Pallas kernels: 141 us -> 138 us
    pallas_call x1, Pallas kernels: 135 us -> 132 us  [local(): pl.pallas_call(kernel, name='afno_backward', out_shape=(jax.ShapeDtypeStr...]
where the time goes in v5:
time: 139 us
  Pallas kernels  138 us (99%)
    pallas_call x1, Pallas kernels, local(): pl.pallas_call(kernel, name='afno_backward', out_shape=(jax.ShapeDtypeStr...  132 us
    pallas_call x1, Pallas kernels, local(): pl.pallas_call(finish, name='finish', out_shape=(jax.ShapeDtypeStruct((LO...  5.99 us

profile of v5, /device:TPU:1, one launch (start us, length us, event | category | flops | bytes accessed | tf_op | source)
XLA Modules:
  0.0 138.7 jit_solution(12867115385524440788)
XLA Ops:
  0.6 132.1 %afno_backward.1 = (bf16[6,384,768]{2,1,0:T(8,128)(2,1)}, bf16[4,2,2,5,32,128]{5,4,3,2,1,0:T(8,128)(2,1)}) custom-call(bf16[6,180,2,768]{3,2,1,0:T(2,128)(2,1)} %bitcast.3, bf16[6,180,2,768]{3,2,1,0:T(2,128)(2,1)} %bitcast.4, f32[2,8,96,96]{3,2,1,0:T(8,128)} %w1.1, f32[2,8,96]{2,1,0:T(8,128)} %b1.1, f32[2,8,96,96]{3,2,1,0:T(8,128)} %w2.1, f32[2,8,96]{2,1,0:T(8,128)} %b2.1, ...), custom_call_target="tpu_custom_call" | custom-call | flops 10000000000 | bytes 10000000 | tf_op jit(solution)/shard_map/afno_backward/pallas_call | solution.py:626
  132.8 6.0 %finish.1 = (bf16[6,180,2,768]{3,2,1,0:T(2,128)(2,1)}, f32[2,8,96,96]{3,2,1,0:T(8,128)}, f32[2,8,96]{2,1,0:T(8,128)}, f32[2,8,96,96]{3,2,1,0:T(8,128)}, f32[2,8,96]{2,1,0:T(8,128)}) custom-call(bf16[4,2,2,5,32,128]{5,4,3,2,1,0:T(8,128)(2,1)} %get-tuple-element.12.every, bf16[6,384,768]{2,1,0:T(8,128)(2,1)} %get-tuple-element.13.grecv, ...), custom_call_target="tpu_custom_call" | custom-call | flops 2000000000 | bytes 8000000 | tf_op jit(solution)/shard_map/finish/pallas_call | solution.py:689

commit v6 on v5

--- a/solution.py
+++ b/solution.py
@@ -86,7 +86,7 @@
     field, cot, w1, b1, w2, b2, tf_hbm, ti_hbm, l1_hbm, l2_hbm, l3_hbm,
     grecv, every,
     slab, send, recv, gsend, mixed, hidden, slope, mask, dsec, dfir, scr, bmat, wm, wtmp, bias, acc, gb,
-    wraw, braw, packed, parts, shares, pieces, done, tf, ti, l1, l2, l3,
+    wraw, braw, packed, parts, shares, pieces, done, whole_ref, tf, ti, l1, l2, l3,
     table_sem, slab_sem, every_sem, par_sem, ssem, rsem, rs_s, rs_r, sum_s, sum_r, all_s, all_r, ag_s, ag_r, pass_s, pass_r,
 ):
     batch, me = lax.axis_index("batch"), lax.axis_index("lat")
@@ -428,7 +428,7 @@
 
     def share(o):
         return pltpu.make_async_remote_copy(
-            packed.at[(batch + o) % BATCH], parts.at[batch], rs_s.at[o], rs_r.at[o],
+            packed.at[(batch + o) % BATCH], parts.at[batch], rs_s, rs_r,
             device_id=((batch + o) % BATCH, me), device_id_type=MESH,
         )
 
@@ -439,11 +439,10 @@
         outward(jc, i).start()
     to_spectra(CHUNKS - 1)
     parts[batch] = packed[batch]
-    for o in range(1, BATCH):
-        dst = parts.at[(batch + BATCH - o) % BATCH]
-        pltpu.make_async_remote_copy(
-            dst, dst, rs_s.at[o], rs_r.at[o], device_id=(batch, me), device_id_type=MESH
-        ).wait_recv()
+    others = parts.at[pl.ds(0, BATCH - 1)]
+    pltpu.make_async_remote_copy(
+        others, others, rs_s, rs_r, device_id=(batch, me), device_id_type=MESH
+    ).wait_recv()
     total = parts[0].astype(F32)
     for o in range(1, BATCH):
         total = total + parts[o].astype(F32)
@@ -453,13 +452,13 @@
 
     def to_reducer(g):
         return pltpu.make_async_remote_copy(
-            shares.at[g], pieces.at[mine], sum_s.at[g], sum_r.at[mine],
+            shares.at[g], pieces.at[mine], sum_s.at[g], sum_r,
             device_id=(batch, half * 8 + g), device_id_type=MESH,
         )
 
     def to_all(i, far):
         return pltpu.make_async_remote_copy(
-            done.at[side, half, mine], done.at[side, half, mine], all_s.at[i, far], all_r.at[side, half, mine],
+            whole_ref, done.at[side, half, mine], all_s.at[far], all_r,
             device_id=((batch, other)[far], index(partner(OFFSETS[i]))), device_id_type=MESH,
         )
 
@@ -476,36 +475,25 @@
     @pl.when(mine < UNITS)
     def _():
         pieces[mine] = shares[mine]
-        for g in range(8):
-
-            @pl.when(mine != g)
-            def _(g=g):
-                dst = pieces.at[g]
-                pltpu.make_async_remote_copy(
-                    dst, dst, sum_s.at[0], sum_r.at[g], device_id=(batch, me), device_id_type=MESH
-                ).wait_recv()
-
+        others = pieces.at[pl.ds(0, 7)]
+        pltpu.make_async_remote_copy(
+            others, others, sum_s.at[0], sum_r, device_id=(batch, me), device_id_type=MESH
+        ).wait_recv()
         whole = pieces[0].astype(F32)
         for g in range(1, 8):
             whole = whole + pieces[g].astype(F32)
         samples = SAMPLES * 2 * NY
-        done[side, half, mine] = (whole * (1.0 / math.sqrt(samples * LAT * (WIDTH // 2 + 1)))).astype(BF16)
+        whole_ref[...] = (whole * (1.0 / math.sqrt(samples * LAT * (WIDTH // 2 + 1)))).astype(BF16)
         for i, far in listeners:
             to_all(i, far).start()
+        pltpu.make_async_copy(whole_ref, done.at[side, half, mine], all_r).start()
 
     for jc, i in back[CUTS[1] : CUTS[2]]:
         outward(jc, i).start()
 
-    for sd in range(2):
-        for hf in range(2):
-            for g in range(UNITS):
-
-                @pl.when((side != sd) | (half != hf) | (mine != g))
-                def _(sd=sd, hf=hf, g=g):
-                    dst = done.at[sd, hf, g]
-                    pltpu.make_async_remote_copy(
-                        dst, dst, all_s.at[0, 0], all_r.at[sd, hf, g], device_id=(batch, me), device_id_type=MESH
-                    ).wait_recv()
+    pltpu.make_async_remote_copy(
+        done, done, all_s.at[0], all_r, device_id=(batch, me), device_id_type=MESH
+    ).wait_recv()
 
     def gathered(o):
         return pltpu.make_async_remote_copy(
@@ -541,8 +529,10 @@
         ).wait_recv()
     kept.wait()
 
-    for o in range(1, BATCH):
-        share(o).wait_send()
+    sent = packed.at[pl.ds(0, BATCH - 1)]
+    pltpu.make_async_remote_copy(
+        sent, sent, rs_s, rs_r, device_id=(batch, me), device_id_type=MESH
+    ).wait_send()
     for o in range(1, NY):
         gathered(o).wait_send()
         passed(o).wait_send()
@@ -554,8 +544,11 @@
 
     @pl.when(mine < UNITS)
     def _():
-        for i, far in listeners:
-            to_all(i, far).wait_send()
+        for far in range(2):
+            sent = mixed.at[pl.ds(0, 32 * (len(OFFSETS) - 1 + far)), pl.ds(0, 128)]
+            pltpu.make_async_remote_copy(
+                sent, sent, all_s.at[far], all_r, device_id=(batch, me), device_id_type=MESH
+            ).wait_send()
 
     for a in range(3):
         for jc in range(CHUNKS):
@@ -618,7 +611,6 @@
     tt = np.ascontiguousarray(tf.T)
     l1, l2, l3 = lat_tables()
     hbm = pl.BlockSpec(memory_space=pl.ANY)
-    n_off = len(OFFSETS)
 
     def pairs(x):
         return x.transpose(1, 2, 0, 3)
@@ -657,6 +649,7 @@
             pltpu.VMEM((UNITS, 32, 128), BF16),
             pltpu.VMEM((8, 32, 128), BF16),
             pltpu.VMEM((2, 2, UNITS, 32, 128), BF16),
+            pltpu.VMEM((32, 128), BF16),
             pltpu.VMEM(tf.shape, BF16),
             pltpu.VMEM(ti.shape, BF16),
             pltpu.VMEM(l1.shape, BF16),
@@ -668,12 +661,12 @@
             pltpu.SemaphoreType.DMA((4,)),
             pltpu.SemaphoreType.DMA((3, CHUNKS)),
             pltpu.SemaphoreType.DMA((3, CHUNKS)),
-            pltpu.SemaphoreType.DMA((BATCH,)),
-            pltpu.SemaphoreType.DMA((BATCH,)),
+            pltpu.SemaphoreType.DMA,
+            pltpu.SemaphoreType.DMA,
             pltpu.SemaphoreType.DMA((UNITS,)),
-            pltpu.SemaphoreType.DMA((8,)),
-            pltpu.SemaphoreType.DMA((n_off, 2)),
-            pltpu.SemaphoreType.DMA((2, 2, UNITS)),
+            pltpu.SemaphoreType.DMA,
+            pltpu.SemaphoreType.DMA((2,)),
+            pltpu.SemaphoreType.DMA,
             pltpu.SemaphoreType.DMA((NY,)),
             pltpu.SemaphoreType.DMA((NY,)),
             pltpu.SemaphoreType.DMA((NY,)),

time: 139 us -> 138 us (level)
  no operation moved by 1% of the time
where the time goes in v6:
time: 138 us
  Pallas kernels  137 us (99%)
    pallas_call x1, Pallas kernels, local(): pl.pallas_call(kernel, name='afno_backward', out_shape=(jax.ShapeDtypeStr...  131 us
    pallas_call x1, Pallas kernels, local(): pl.pallas_call(finish, name='finish', out_shape=(jax.ShapeDtypeStruct((LO...  5.99 us

profile of v6, /device:TPU:1, one launch (start us, length us, event | category | flops | bytes accessed | tf_op | source)
XLA Modules:
  0.0 138.1 jit_solution(8638989215382513297)
XLA Ops:
  0.6 131.4 %afno_backward.1 = (bf16[6,384,768]{2,1,0:T(8,128)(2,1)}, bf16[4,2,2,5,32,128]{5,4,3,2,1,0:T(8,128)(2,1)}) custom-call(bf16[6,180,2,768]{3,2,1,0:T(2,128)(2,1)} %bitcast.3, bf16[6,180,2,768]{3,2,1,0:T(2,128)(2,1)} %bitcast.4, f32[2,8,96,96]{3,2,1,0:T(8,128)} %w1.1, f32[2,8,96]{2,1,0:T(8,128)} %b1.1, f32[2,8,96,96]{3,2,1,0:T(8,128)} %w2.1, f32[2,8,96]{2,1,0:T(8,128)} %b2.1, ...), custom_call_target="tpu_custom_call" | custom-call | flops 10000000000 | bytes 10000000 | tf_op jit(solution)/shard_map/afno_backward/pallas_call | solution.py:618
  132.1 6.0 %finish.1 = (bf16[6,180,2,768]{3,2,1,0:T(2,128)(2,1)}, f32[2,8,96,96]{3,2,1,0:T(8,128)}, f32[2,8,96]{2,1,0:T(8,128)}, f32[2,8,96,96]{3,2,1,0:T(8,128)}, f32[2,8,96]{2,1,0:T(8,128)}) custom-call(bf16[4,2,2,5,32,128]{5,4,3,2,1,0:T(8,128)(2,1)} %get-tuple-element.12.every, bf16[6,384,768]{2,1,0:T(8,128)(2,1)} %get-tuple-element.13.grecv, ...), custom_call_target="tpu_custom_call" | custom-call | flops 2000000000 | bytes 8000000 | tf_op jit(solution)/shard_map/finish/pallas_call | solution.py:682
